TPU v7x, 32 devices: a whole 2x2x4 slice. The times are simulated.
32 devices in a mesh: dp: 8 (over z, x), seq: 2 (over core), sect: 2 (over y).
Axes of the slice: x: 2, y: 2, z: 4, core: 2. Of those that a mesh axis runs over, the one named last changes fastest.
Arguments:
- bases: int32 [16, 512], P(('dp', 'sect'), 'seq'), may hold values from 0 to 3
- embed: bfloat16 [5, 4, 384], replicated, may hold values from -2.5 to 2.5
- conv_w: bfloat16 [5, 384, 384], P(None, 'seq'), may hold values from -0.125 to 0.125
- w_in: bfloat16 [384, 768], P('seq', 'sect'), may hold values from -0.3125 to 0.3125
- w_out: bfloat16 [768, 384], P('sect', 'seq'), may hold values from -0.21875 to 0.21875
- cotangent: bfloat16 [16, 512, 384], P(('dp', 'sect'), 'seq'), may hold values from -0.15625 to 0.15625
Outputs:
- output: bfloat16 [16, 512, 384], P(('dp', 'sect'), 'seq')
- grad_embed: float32 [5, 4, 384], P(None, None, 'seq')
- grad_conv: float32 [5, 384, 384], P(None, 'seq')
- grad_in: float32 [384, 768], P('seq', 'sect')
- grad_out: float32 [768, 384], P('sect', 'seq')
All inputs are finite; a program needn't handle non-finite values.
Results may differ from a plain program's by a relative error of at most 0.0088.
Values may be sent and summed in bfloat16 or wider, within the bound.
A program may use at most 64 MiB of HBM per device.

v0:
```python
import jax
import jax.numpy as jnp
from jax import lax
from jax.sharding import PartitionSpec as P

TAPS = 5
BASES = 4


def swapped(value, axis, apart):
    mask = 2**apart
    pairs = [(source, source ^ mask) for source in range(lax.axis_size(axis))]
    return lax.ppermute(value, axis, pairs)


def padded(cells, sides, width):
    for axis, dim in sides:
        count = lax.axis_size(axis)
        ends = count - 1
        head = lax.slice_in_dim(cells, 0, width, axis=dim)
        tail = lax.slice_in_dim(cells, cells.shape[dim] - width, cells.shape[dim], axis=dim)
        cells = jnp.concatenate(
            [
                lax.ppermute(tail, axis, [(i, (i + 1) % count) for i in range(ends)]),
                cells,
                lax.ppermute(head, axis, [((i + 1) % count, i) for i in range(ends)]),
            ],
            axis=dim,
        )
    return cells


def gelu_tanh(value):
    return jax.nn.gelu(value, approximate=True)


def gelu_back(value, grad):
    unused, pull = jax.vjp(gelu_tanh, value)
    return pull(grad)[0]


def contract_rows(left, right):
    return lax.dot_general(
        left, right, (((0,), (0,)), ((), ())), preferred_element_type=jnp.float32
    )


def contract_cols(left, right):
    return lax.dot_general(
        left, right, (((1,), (1,)), ((), ())), preferred_element_type=jnp.float32
    )


def partner_rows(value):
    return swapped(value, "sect", 0)


def partner_sums(value):
    return swapped(value.astype(jnp.bfloat16), "sect", 0).astype(value.dtype)


def local(bases, embed, conv_w, w_in, w_out, cotangent):
    rows = bases.shape[1]
    chans = embed.shape[2]
    half = rows // 2
    padded_ids = padded(bases[0] + 1, (("seq", 0),), 2)
    levels = jnp.arange(1, BASES + 1, dtype=jnp.int32)
    onehots = [
        (padded_ids[k : k + rows, None] == levels[None, :]).astype(jnp.bfloat16)
        for k in range(TAPS)
    ]
    accum = jnp.zeros((rows, chans), jnp.float32)
    for k in range(TAPS):
        accum = accum + jnp.dot(onehots[k], embed[k], preferred_element_type=jnp.float32)
    h_zero = accum.astype(jnp.bfloat16)
    conv_full = lax.all_gather(conv_w, "seq", axis=1, tiled=True)
    h_padded = padded(h_zero, (("seq", 0),), 2)
    pre_conv = jnp.zeros((rows, chans), jnp.float32)
    for k in range(TAPS):
        pre_conv = pre_conv + jnp.dot(
            h_padded[k : k + rows], conv_full[k], preferred_element_type=jnp.float32
        )
    h_one = lax.optimization_barrier(
        (h_zero.astype(jnp.float32) + gelu_tanh(pre_conv)).astype(jnp.bfloat16)
    )
    h_onef = h_one.astype(jnp.float32)
    pooled = lax.optimization_barrier(
        (h_onef.reshape(half, 2, chans).sum(1) * 0.5).astype(jnp.bfloat16)
    )
    pooledf = pooled.astype(jnp.float32)
    scale = lax.rsqrt(jnp.mean(pooledf * pooledf, axis=-1, keepdims=True) + 1e-06)
    normed = (pooledf * scale).astype(jnp.bfloat16)
    in_rows, out_cols = (
        lax.all_gather(w_in, "seq", axis=0, tiled=True),
        lax.all_gather(w_out, "seq", axis=1, tiled=True),
    )
    dout = cotangent[0].astype(jnp.float32)
    dmixed = dout.reshape(half, 2, chans).sum(1).astype(jnp.bfloat16)
    both = jnp.concatenate([normed, partner_rows(normed)], axis=0)
    pre = jnp.dot(both, in_rows, preferred_element_type=jnp.float32)
    act = gelu_tanh(pre).astype(jnp.bfloat16)
    partial_value = jnp.dot(act, out_cols, preferred_element_type=jnp.float32)
    mixed = lax.optimization_barrier(
        (partial_value[:half] + partner_sums(partial_value[half:])).astype(jnp.bfloat16)
    )
    dmixed_both = jnp.concatenate([dmixed, partner_rows(dmixed)], axis=0)
    out_term = contract_rows(act, dmixed_both)
    dact = contract_cols(dmixed_both, out_cols)
    dpre = gelu_back(pre, dact).astype(jnp.bfloat16)
    in_term = contract_rows(both, dpre)
    dnormed_part = contract_cols(dpre, in_rows)
    dnormed = dnormed_part[:half] + partner_sums(dnormed_part[half:])
    in_share, out_share = (
        lax.psum_scatter(in_term, "seq", scatter_dimension=0, tiled=True),
        lax.psum_scatter(out_term, "seq", scatter_dimension=1, tiled=True),
    )
    grad_in, grad_out = lax.psum((in_share, out_share), "dp")
    output = (h_onef + jnp.repeat(mixed.astype(jnp.float32), 2, axis=0)).astype(jnp.bfloat16)
    dpooled = scale * dnormed - pooledf * scale**3 * jnp.mean(
        dnormed * pooledf, axis=-1, keepdims=True
    )
    dh_one = dout + jnp.repeat(dpooled * 0.5, 2, axis=0)
    dz_rows = gelu_back(pre_conv, dh_one).astype(jnp.bfloat16)
    dz_padded = padded(dz_rows, (("seq", 0),), 2)
    dh_zero = dh_one
    for k in range(TAPS):
        dh_zero = dh_zero + contract_cols(dz_padded[4 - k : 4 - k + rows], conv_full[k])
    conv_term = jnp.stack([contract_rows(h_padded[k : k + rows], dz_rows) for k in range(TAPS)])
    embed_term = jnp.stack(
        [
            lax.dot_general(
                onehots[k].astype(jnp.float32),
                dh_zero,
                (((0,), (0,)), ((), ())),
                precision=lax.Precision.HIGHEST,
                preferred_element_type=jnp.float32,
            )
            for k in range(TAPS)
        ]
    )
    conv_share, embed_share = (
        lax.psum_scatter(conv_term, "seq", scatter_dimension=1, tiled=True),
        lax.psum_scatter(embed_term, "seq", scatter_dimension=2, tiled=True),
    )
    grad_conv, grad_embed = lax.psum((conv_share, embed_share), ("dp", "sect"))
    return (output[None], grad_embed, grad_conv, grad_in, grad_out)


def solution(mesh):
    placed = (
        P(("dp", "sect"), "seq"),
        P(),
        P(None, "seq", None),
        P("seq", "sect"),
        P("sect", "seq"),
        P(("dp", "sect"), "seq", None),
    )
    return jax.shard_map(
        local,
        mesh=mesh,
        in_specs=placed,
        out_specs=(
            P(("dp", "sect"), "seq", None),
            P(None, None, "seq"),
            P(None, "seq", None),
            P("seq", "sect"),
            P("sect", "seq"),
        ),
        check_vma=False,
    )
```

profile of v0, /device:TPU:0, one launch (start us, length us, event | category | flops | bytes accessed | tf_op | source)
XLA Modules:
  0.0 293.9 jit_solution(17406500528449649902)
XLA Ops:
  7.2 0.7 all-gather.2.cloned.1.call-update
  8.0 0.7 broadcast_add_fusion
  8.7 1.3 collective-permute-start.1
  10.0 3.0 %collective-permute-start = (s32[2]{0:T(128)S(1)}, s32[2]{0:T(128)S(1)}, u32[]{:S(2)}, u32[]{:S(2)}) collective-permute-start(s32[2]{0:T(128)S(1)} %get-tuple-element.18), channel_id=1, source_target_pairs={{0,2},{1,3},{4,6},{5,7},{8,10},{9,11},{12,14},{13,15},{16,18},{17,... | collective-permute-start | bytes 32 | tf_op jit(solution)/shard_map/ppermute | solution.py:24
  13.1 0.8 collective-permute-done
  14.0 0.9 fusion.61
  14.9 0.9 convolution_add_fusion.7
  16.7 2.2 collective-permute-start.2
  19.0 1.3 collective-permute-start.3
  20.3 1.7 all-gather.2.cloned.1.call-done
  22.0 1.3 fusion.33
  23.3 1.2 fusion.35
  25.1 0.4 add_convert_fusion.1
  25.7 0.5 reduce_sum.39
  26.3 0.6 multiply_multiply_fusion.4
  27.0 0.5 copy-done.17
  27.6 1.9 collective-permute-start.4
  29.5 0.5 reduce_sum.41
  30.0 0.3 collective-permute-start.6
  30.3 2.2 all_gather.10
  32.5 0.5 collective-permute-done.4
  33.3 1.8 collective-permute-done.6
  35.2 0.6 copy-done.20
  35.8 1.2 fusion.63
  37.1 2.2 all_gather.11
  39.3 1.4 fusion.29
  40.7 0.3 fusion.118
  41.0 1.8 collective-permute-start.7
  42.9 1.1 fusion.65
  44.0 1.9 collective-permute-done.7
  46.7 0.3 fusion.22
  47.0 1.1 fusion.4
  48.1 1.1 fusion.3
  49.2 1.1 fusion.2
  50.3 1.1 fusion.1
  51.4 1.1 fusion
  52.7 1.3 collective-permute-start.8
  54.0 3.0 %collective-permute-start.9 = (bf16[2,384]{1,0:T(2,128)(2,1)S(1)}, bf16[2,384]{1,0:T(2,128)(2,1)S(1)}, u32[]{:S(2)}, u32[]{:S(2)}) collective-permute-start(bf16[2,384]{1,0:T(2,128)(2,1)S(1)} %get-tuple-element.8), channel_id=1, source_target_pairs={{0,2},{1,3},{4,6},{5,7},{8,10},{9,11},{12,14},{13,15},{16,18},{17,... | collective-permute-start | bytes 4616 | tf_op jit(solution)/shard_map/ppermute | solution.py:24
  57.0 0.3 fusion.32
  57.3 0.5 collective-permute-done.9
  57.8 0.3 fusion.34
  58.1 0.3 fusion.30
  58.4 0.3 fusion.8
  58.8 0.3 fusion.9
  59.1 0.3 fusion.15
  59.4 0.3 fusion.14
  59.8 0.3 fusion.13
  60.1 0.3 fusion.12
  60.4 0.3 fusion.11
  60.8 0.6 copy.11
  61.4 1.0 reshape.62
  62.5 0.5 all-reduce.6.cloned.1.call-update
  63.0 9.7 %reduce-scatter.7.cloned.1.call-done = f32[5,192,384]{2,1,0:T(8,128)} async-done(((f32[5,384,384]{2,1,0:T(8,128)}), f32[5,192,384]{2,1,0:T(8,128)}) %reduce-scatter.7.cloned.1.call-update) | async-done | bytes 1474576 | tf_op jit(solution)/shard_map/reduce_scatter | solution.py:142
  72.7 0.3 fusion.113
  73.1 1.9 collective-permute-start.5
  75.0 3.2 %collective-permute-done.5 = bf16[128,384]{1,0:T(8,128)(2,1)S(1)} collective-permute-done((bf16[128,384]{1,0:T(8,128)(2,1)S(1)}, bf16[128,384]{1,0:T(8,128)(2,1)S(1)}, u32[]{:S(2)}, u32[]{:S(2)}) %collective-permute-start.5) | collective-permute-done | bytes 98336 | tf_op jit(solution)/shard_map/ppermute | solution.py:13
  78.6 0.7 fusion.48
  79.3 5.0 %reduce-scatter.13.cloned.1.call-done = f32[192,20]{1,0:T(8,128)} async-done(((f32[384,20]{1,0:T(8,128)}), f32[192,20]{1,0:T(8,128)}) %reduce-scatter.13.cloned.1.call-update) | async-done | bytes 15376
  84.3 1.1 reshape.63
  85.6 77.2 %psum.28 = f32[5,4,192]{2,1,0:T(4,128)} all-reduce(f32[5,4,192]{2,1,0:T(4,128)S(1)} %copy.12), channel_id=1, replica_groups=mesh['dp'=8,'seq'=2,'sect'=2] {'dp','sect'}, use_global_device_ids=true, to_apply=%region_5.0 | all-reduce | flops 3840 | bytes 30720 | tf_op jit(solution)/shard_map/psum | solution.py:145
  162.8 120.2 %all-reduce.4.cloned.1.call-done = f32[5,192,384]{2,1,0:T(8,128)} async-done(((f32[5,192,384]{2,1,0:T(8,128)}), f32[5,192,384]{2,1,0:T(8,128)}) %all-reduce.4.cloned.1.call-update) | async-done | bytes 1474576 | tf_op jit(solution)/shard_map/psum | solution.py:145
  283.0 2.6 copy.24
  285.7 0.7 copy.25
  286.4 0.7 copy.26
  (87 shorter events, 4.1 us)
Async XLA Ops:
  7.2 8.7 %copy-start.8 = (bf16[5,4,384]{2,1,0:T(4,128)(2,1)S(1)}, bf16[5,4,384]{2,1,0:T(4,128)(2,1)}, u32[]{:S(2)}) copy-start(bf16[5,4,384]{2,1,0:T(4,128)(2,1)} %param.7) | copy-start | bytes 46084
  7.2 14.8 %all-gather.2.cloned.1.call-start = ((), (), s32[]{:S(2)}) async-start(), calls=%async_computation.4 | async-start | bytes 2211840 | tf_op jit(solution)/shard_map/all_gather | solution.py:76
  7.9 54.5 %reduce-scatter.11.cloned.1.call-start = ((), (), s32[]{:S(2)}) async-start(), calls=%async_computation.8 | async-start | bytes 884736 | tf_op jit(solution)/shard_map/reduce_scatter | solution.py:115
  8.7 4.3 %collective-permute-start.1 = (s32[2]{0:T(128)S(1)}, s32[2]{0:T(128)S(1)}, u32[]{:S(2)}, u32[]{:S(2)}) collective-permute-start(s32[2]{0:T(128)S(1)} %get-tuple-element.17), channel_id=1, source_target_pairs={{2,0},{3,1},{6,4},{7,5},{10,8},{11,9},{14,12},{15,13},{18,16},{19,... | collective-permute-start | bytes 32 | tf_op jit(solution)/shard_map/ppermute | solution.py:26
  10.0 3.8 %collective-permute-start = (s32[2]{0:T(128)S(1)}, s32[2]{0:T(128)S(1)}, u32[]{:S(2)}, u32[]{:S(2)}) collective-permute-start(s32[2]{0:T(128)S(1)} %get-tuple-element.18), channel_id=1, source_target_pairs={{0,2},{1,3},{4,6},{5,7},{8,10},{9,11},{12,14},{13,15},{16,18},{17,... | collective-permute-start | bytes 32 | tf_op jit(solution)/shard_map/ppermute | solution.py:24
  14.0 2.7 copy-start.9
  14.0 2.7 copy-start.11
  14.0 2.7 copy-start.13
  14.0 2.7 copy-start.15
  16.7 7.8 %collective-permute-start.2 = (bf16[2,384]{1,0:T(2,128)(2,1)S(1)}, bf16[2,384]{1,0:T(2,128)(2,1)S(1)}, u32[]{:S(2)}, u32[]{:S(2)}) collective-permute-start(bf16[2,384]{1,0:T(2,128)(2,1)S(1)} %get-tuple-element.9), channel_id=1, source_target_pairs={{0,2},{1,3},{4,6},{5,7},{8,10},{9,11},{12,14},{13,15},{16,18},{17,... | collective-permute-start | bytes 4616 | tf_op jit(solution)/shard_map/ppermute | solution.py:24
  19.0 4.3 %collective-permute-start.3 = (bf16[2,384]{1,0:T(2,128)(2,1)S(1)}, bf16[2,384]{1,0:T(2,128)(2,1)S(1)}, u32[]{:S(2)}, u32[]{:S(2)}) collective-permute-start(bf16[2,384]{1,0:T(2,128)(2,1)S(1)} %get-tuple-element.10), channel_id=1, source_target_pairs={{2,0},{3,1},{6,4},{7,5},{10,8},{11,9},{14,12},{15,13},{18,16},{19,... | collective-permute-start | bytes 4616 | tf_op jit(solution)/shard_map/ppermute | solution.py:26
  21.9 2.6 copy-start
  25.1 4.3 %copy-start.1 = (bf16[1,256,384]{2,1,0:T(8,128)(2,1)S(1)}, bf16[1,256,384]{2,1,0:T(8,128)(2,1)}, u32[]{:S(2)}) copy-start(bf16[1,256,384]{2,1,0:T(8,128)(2,1)} %param.11) | copy-start | bytes 589828
  27.0 0.5 copy-start.17
  27.6 5.5 %collective-permute-start.4 = (bf16[128,384]{1,0:T(8,128)(2,1)S(1)}, bf16[128,384]{1,0:T(8,128)(2,1)S(1)}, u32[]{:S(2)}, u32[]{:S(2)}) collective-permute-start(bf16[128,384]{1,0:T(8,128)(2,1)S(1)} %fusion.43), channel_id=1, source_target_pairs={{0,1},{1,0},{2,3},{3,2},{4,5},{5,4},{6,7},{7,6},{8,9},{9,8},{10,11... | collective-permute-start | bytes 294920 | tf_op jit(solution)/shard_map/ppermute | solution.py:13
  30.0 5.1 %collective-permute-start.6 = (bf16[128,384]{1,0:T(8,128)(2,1)S(1)}, bf16[128,384]{1,0:T(8,128)(2,1)S(1)}, u32[]{:S(2)}, u32[]{:S(2)}) collective-permute-start(bf16[128,384]{1,0:T(8,128)(2,1)S(1)} %reduce_sum.41), channel_id=1, source_target_pairs={{0,1},{1,0},{2,3},{3,2},{4,5},{5,4},{6,7},{7,6},{8,9},{9,8},{10,11... | collective-permute-start | bytes 294920 | tf_op jit(solution)/shard_map/ppermute | solution.py:13
  33.3 6.0 %copy-start.2 = (f32[256,384]{1,0:T(8,128)}, f32[256,384]{1,0:T(8,128)S(1)}, u32[]{:S(2)}) copy-start(f32[256,384]{1,0:T(8,128)S(1)} %fusion.66) | copy-start | bytes 1179652
  35.2 0.6 copy-start.20
  37.0 25.4 %reduce-scatter.9.cloned.1.call-start = ((), (), s32[]{:S(2)}) async-start(), calls=%async_computation.7 | async-start | bytes 884736 | tf_op jit(solution)/shard_map/reduce_scatter | solution.py:114
  39.3 1.7 copy-start.4
  40.7 5.4 %copy-start.18 = (f32[128]{0:T(128)S(1)}, f32[128]{0:T(128)}, u32[]{:S(2)}) copy-start(f32[128]{0:T(128)} %copy-done.17) | copy-start | bytes 1540
  40.7 5.4 %copy-start.19 = (f32[128]{0:T(128)S(1)}, f32[128]{0:T(128)}, u32[]{:S(2)}) copy-start(f32[128]{0:T(128)} %get-tuple-element.19) | copy-start | bytes 1540
  41.0 4.9 %collective-permute-start.7 = (bf16[128,384]{1,0:T(8,128)(2,1)S(1)}, bf16[128,384]{1,0:T(8,128)(2,1)S(1)}, u32[]{:S(2)}, u32[]{:S(2)}) collective-permute-start(bf16[128,384]{1,0:T(8,128)(2,1)S(1)} %slice.265), channel_id=1, source_target_pairs={{0,1},{1,0},{2,3},{3,2},{4,5},{5,4},{6,7},{7,6},{8,9},{9,8},{10,11... | collective-permute-start | bytes 294920 | tf_op jit(solution)/shard_map/ppermute | solution.py:13
  44.0 28.7 %reduce-scatter.7.cloned.1.call-start = ((), (), s32[]{:S(2)}) async-start(), calls=%async_computation.5 | async-start | bytes 4423680 | tf_op jit(solution)/shard_map/reduce_scatter | solution.py:142
  52.6 31.7 %reduce-scatter.13.cloned.1.call-start = ((), (), s32[]{:S(2)}) async-start(), calls=%async_computation.9 | async-start | bytes 294912
  52.7 5.4 %collective-permute-start.8 = (bf16[2,384]{1,0:T(2,128)(2,1)S(1)}, bf16[2,384]{1,0:T(2,128)(2,1)S(1)}, u32[]{:S(2)}, u32[]{:S(2)}) collective-permute-start(bf16[2,384]{1,0:T(2,128)(2,1)S(1)} %get-tuple-element.7), channel_id=1, source_target_pairs={{2,0},{3,1},{6,4},{7,5},{10,8},{11,9},{14,12},{15,13},{18,16},{19,... | collective-permute-start | bytes 4616 | tf_op jit(solution)/shard_map/ppermute | solution.py:26
  54.0 3.8 %collective-permute-start.9 = (bf16[2,384]{1,0:T(2,128)(2,1)S(1)}, bf16[2,384]{1,0:T(2,128)(2,1)S(1)}, u32[]{:S(2)}, u32[]{:S(2)}) collective-permute-start(bf16[2,384]{1,0:T(2,128)(2,1)S(1)} %get-tuple-element.8), channel_id=1, source_target_pairs={{0,2},{1,3},{4,6},{5,7},{8,10},{9,11},{12,14},{13,15},{16,18},{17,... | collective-permute-start | bytes 4616 | tf_op jit(solution)/shard_map/ppermute | solution.py:24
  58.4 0.7 copy-start.16
  58.8 0.7 copy-start.14
  58.8 1.3 copy-start.12
  58.8 1.7 copy-start.10
  62.3 10.4 %copy-start.3 = (f32[256,384]{1,0:T(8,128)S(1)}, f32[256,384]{1,0:T(8,128)}, u32[]{:S(2)}) copy-start(f32[256,384]{1,0:T(8,128)} %copy-done.2) | copy-start | bytes 1179652
  62.3 10.4 %copy-start.5 = (bf16[384,384]{0,1:T(8,128)(2,1)S(1)}, bf16[384,384]{0,1:T(8,128)(2,1)}, u32[]{:S(2)}) copy-start(bf16[384,384]{0,1:T(8,128)(2,1)} %copy-done.4) | copy-start | bytes 884740
  62.4 100.4 %all-reduce.6.cloned.1.call-start = ((), (), s32[]{:S(2)}) async-start(), calls=%async_computation.10 | async-start | bytes 1179648 | tf_op jit(solution)/shard_map/psum | solution.py:117
  62.9 220.1 %all-reduce.4.cloned.1.call-start = ((), (), s32[]{:S(2)}) async-start(), calls=%async_computation.6 | async-start | bytes 2949120 | tf_op jit(solution)/shard_map/psum | solution.py:145
  73.1 5.1 %collective-permute-start.5 = (bf16[128,384]{1,0:T(8,128)(2,1)S(1)}, bf16[128,384]{1,0:T(8,128)(2,1)S(1)}, u32[]{:S(2)}, u32[]{:S(2)}) collective-permute-start(bf16[128,384]{1,0:T(8,128)(2,1)S(1)} %slice.266), channel_id=1, source_target_pairs={{0,1},{1,0},{2,3},{3,2},{4,5},{5,4},{6,7},{7,6},{8,9},{9,8},{10,11... | collective-permute-start | bytes 294920 | tf_op jit(solution)/shard_map/ppermute | solution.py:13
  283.0 2.6 copy-start.7
  283.0 3.4 %copy-start.6 = (f32[384,192]{0,1:T(8,128)S(1)}, f32[384,192]{0,1:T(8,128)}, u32[]{:S(2)}) copy-start(f32[384,192]{0,1:T(8,128)} %get-tuple-element.29) | copy-start | bytes 884740
Sparse Core Ops, SparseCore 0:
  9.6 12.3 all-gather.1
  37.2 9.4 reduce-scatter.10
  49.6 9.1 reduce-scatter.8
  61.0 11.6 reduce-scatter.6
  75.4 8.8 reduce-scatter.12
  87.9 74.3 all-reduce.5
  167.8 115.1 all-reduce.3
where the time goes:
time: 294 us
  waiting for transfers between devices  147 us (50%)
  blocking collectives  81.6 us (28%)
  matrix products  19.5 us (7%)
  starting transfers between devices  18.3 us (6%)
  between operations  14.7 us (5%)
  local copies, waits for them, and re-layouts  9.46 us (3%)
  other arithmetic  3.81 us (1%)
    psum x1, waiting for transfers between devices, local(): grad_conv, grad_embed = lax.psum((conv_share, embed_share), ('dp', 'sect'))  120 us
    psum x1, blocking collectives, local(): grad_conv, grad_embed = lax.psum((conv_share, embed_share), ('dp', 'sect'))  77.2 us
    reduce_scatter x1, waiting for transfers between devices, local(): lax.psum_scatter(conv_term, 'seq', scatter_dimension=1, tiled=True)  9.71 us
    ppermute x3, starting transfers between devices, padded(): lax.ppermute(tail, axis, [(i, (i + 1) % count) for i in range(ends)])  8.26 us
    unnamed x49, local copies, waits for them, and re-layouts  8.22 us
    dot_general x7, matrix products, contract_rows(): lax.dot_general(left, right, (((0,), (0,)), ((), ())), preferred_element_...  7.92 us
    ppermute x4, waiting for transfers between devices, swapped(): return lax.ppermute(value, axis, pairs)  7.45 us
    unnamed x8, waiting for transfers between devices  6.23 us
  transfers between devices with their start and end apart: 17, of which 10 were waited for; matrix products, arithmetic and copies ran while one was open for 8% of the time, Pallas kernels for 0%

commit v1 on v0

--- a/solution.py
+++ b/solution.py
@@ -1,6 +1,10 @@
+import functools
+
 import jax
 import jax.numpy as jnp
 from jax import lax
+from jax.experimental import pallas as pl
+from jax.experimental.pallas import tpu as pltpu
 from jax.sharding import PartitionSpec as P
 
 TAPS = 5
@@ -57,6 +61,271 @@
 
 def partner_sums(value):
     return swapped(value.astype(jnp.bfloat16), "sect", 0).astype(value.dtype)
+
+
+def remote(src, dst, send, recv, place):
+    return pltpu.make_async_remote_copy(
+        src_ref=src,
+        dst_ref=dst,
+        send_sem=send,
+        recv_sem=recv,
+        device_id=place,
+        device_id_type=pl.DeviceIdType.MESH,
+    )
+
+
+def reduce_kernel(
+    seqs, high, conv_in, feed_in, conv_out, feed_out,
+    conv_r0, feed_r0, conv_a1, feed_a1, conv_r1, feed_r1, conv_a2, feed_a2,
+    conv_r2, feed_r2, conv_all, feed_all,
+    s0, r0, s1, r1, s2, r2, s3, r3, s4, r4,
+):
+    me_seq = lax.axis_index("seq")
+    me_sect = lax.axis_index("sect")
+    me_dp = lax.axis_index("dp")
+    low = lax.rem(me_dp, 2)
+    up = me_dp // 2
+    quad = me_sect * 2 + low
+    conv_block, feed_block = conv_a2.shape[0], feed_a2.shape[0]
+    conv_piece, feed_piece = conv_r2.shape[1], feed_r2.shape[1]
+
+    seq_ids = [lax.rem(me_seq + k, seqs) for k in range(1, seqs)]
+    quad_ids = [(k // 2, k % 2) for k in range(1, 4)]
+    quad_ids = [
+        (lax.rem(me_sect + a, 2), lax.rem(low + b, 2)) for a, b in quad_ids
+    ]
+    high_ids = [lax.rem(up + k, high) for k in range(1, high)]
+    seq_place = [{"seq": p} for p in seq_ids]
+    quad_place = [{"sect": a, "dp": up * 2 + b} for a, b in quad_ids]
+    high_place = [{"dp": p * 2 + low} for p in high_ids]
+
+    barrier = pltpu.get_barrier_semaphore()
+    for place in seq_place + quad_place + high_place:
+        pl.semaphore_signal(
+            barrier, inc=1, device_id=place, device_id_type=pl.DeviceIdType.MESH
+        )
+    pl.semaphore_wait(barrier, len(seq_place) + len(quad_place) + len(high_place))
+
+    def rows(index, size):
+        return pl.ds(pl.multiple_of(index * size, size), size)
+
+    def finish(copies):
+        for copy in copies:
+            copy.wait_recv()
+        for copy in copies:
+            copy.wait_send()
+
+    def total(count, size, dest, own, slots):
+        def body(i, carry):
+            at = rows(i, size)
+            value = own(at).astype(jnp.float32)
+            for slot in range(slots.shape[0]):
+                value = value + slots[slot, at].astype(jnp.float32)
+            dest[at] = value.astype(dest.dtype)
+            return carry
+
+        lax.fori_loop(0, count, body, 0)
+
+    copies = []
+    for k in range(seqs - 1):
+        copies.append(
+            remote(conv_in.at[seq_ids[k]], conv_r0.at[k], s0.at[0, k], r0.at[0, k], seq_place[k])
+        )
+        copies.append(
+            remote(feed_in.at[seq_ids[k]], feed_r0.at[k], s0.at[1, k], r0.at[1, k], seq_place[k])
+        )
+    for copy in copies:
+        copy.start()
+    finish(copies)
+    total(4 * high, conv_piece, conv_a1, lambda at: conv_in[me_seq, at], conv_r0)
+    total(2 * high, feed_piece, feed_a1, lambda at: feed_in[me_seq, at], feed_r0)
+
+    copies = []
+    for k in (2, 1, 0):
+        a, b = quad_ids[k]
+        copies.append(
+            remote(
+                conv_a1.at[rows(a * 2 + b, conv_block)],
+                conv_r1.at[k],
+                s1.at[k],
+                r1.at[k],
+                quad_place[k],
+            )
+        )
+    copies.append(
+        remote(
+            feed_a1.at[rows(quad_ids[0][1], feed_block)],
+            feed_r1.at[0],
+            s1.at[3],
+            r1.at[3],
+            quad_place[0],
+        )
+    )
+    for copy in copies:
+        copy.start()
+    finish(copies)
+    conv_at, feed_at = quad * conv_block, low * feed_block
+
+    def own_conv(at):
+        return conv_a1[pl.ds(pl.multiple_of(conv_at + at.start, conv_piece), conv_piece)]
+
+    def own_feed(at):
+        return feed_a1[pl.ds(pl.multiple_of(feed_at + at.start, feed_piece), feed_piece)]
+
+    total(high, conv_piece, conv_a2, own_conv, conv_r1)
+    total(high, feed_piece, feed_a2, own_feed, feed_r1)
+
+    copies = []
+    for k in range(high - 1):
+        copies.append(
+            remote(
+                conv_a2.at[rows(high_ids[k], conv_piece)],
+                conv_r2.at[k],
+                s2.at[0, k],
+                r2.at[0, k],
+                high_place[k],
+            )
+        )
+        copies.append(
+            remote(
+                feed_a2.at[rows(high_ids[k], feed_piece)],
+                feed_r2.at[k],
+                s2.at[1, k],
+                r2.at[1, k],
+                high_place[k],
+            )
+        )
+    for copy in copies:
+        copy.start()
+    finish(copies)
+    conv_mine = rows(quad * high + up, conv_piece)
+    feed_mine = rows(low * high + up, feed_piece)
+    value = conv_a2[rows(up, conv_piece)].astype(jnp.float32)
+    for k in range(high - 1):
+        value = value + conv_r2[k].astype(jnp.float32)
+    conv_all[conv_mine] = value.astype(jnp.bfloat16)
+    value = feed_a2[rows(up, feed_piece)].astype(jnp.float32)
+    for k in range(high - 1):
+        value = value + feed_r2[k].astype(jnp.float32)
+    feed_all[feed_mine] = value.astype(jnp.bfloat16)
+
+    copies = []
+    for k in range(high - 1):
+        copies.append(
+            remote(
+                conv_all.at[conv_mine], conv_all.at[conv_mine],
+                s3.at[0, k], r3.at[0, k], high_place[k],
+            )
+        )
+        copies.append(
+            remote(
+                feed_all.at[feed_mine], feed_all.at[feed_mine],
+                s3.at[1, k], r3.at[1, k], high_place[k],
+            )
+        )
+    for copy in copies:
+        copy.start()
+    finish(copies)
+
+    copies = []
+    for k in (2, 1, 0):
+        mine = conv_all.at[rows(quad, conv_block)]
+        copies.append(remote(mine, mine, s4.at[k], r4.at[k], quad_place[k]))
+    mine = feed_all.at[rows(low, feed_block)]
+    copies.append(remote(mine, mine, s4.at[3], r4.at[3], quad_place[0]))
+    for copy in copies:
+        copy.start()
+    finish(copies)
+
+    def widen(count, size, dest, source):
+        def body(i, carry):
+            at = rows(i, size)
+            dest[at] = source[at].astype(jnp.float32)
+            return carry
+
+        lax.fori_loop(0, count, body, 0)
+
+    widen(4 * high, conv_piece, conv_out, conv_all)
+    widen(2 * high, feed_piece, feed_out, feed_all)
+
+
+def summed(conv_pack, feed_pack):
+    seqs = lax.axis_size("seq")
+    high = lax.axis_size("dp") // 2
+    conv_rows, feed_rows, cols = conv_pack.shape[1], feed_pack.shape[1], conv_pack.shape[2]
+    conv_block, feed_block = conv_rows // 4, feed_rows // 2
+    conv_piece, feed_piece = conv_block // high, feed_block // high
+    low = jnp.bfloat16
+
+    def buffer(*shape):
+        return pltpu.VMEM(shape + (cols,), low)
+
+    dma = pltpu.SemaphoreType.DMA
+    return pl.pallas_call(
+        functools.partial(reduce_kernel, seqs, high),
+        out_shape=(
+            jax.ShapeDtypeStruct((conv_rows, cols), jnp.float32),
+            jax.ShapeDtypeStruct((feed_rows, cols), jnp.float32),
+        ),
+        in_specs=[pl.BlockSpec(memory_space=pltpu.VMEM)] * 2,
+        out_specs=[pl.BlockSpec(memory_space=pltpu.VMEM)] * 2,
+        scratch_shapes=[
+            buffer(seqs - 1, conv_rows),
+            buffer(seqs - 1, feed_rows),
+            buffer(conv_rows),
+            buffer(feed_rows),
+            buffer(3, conv_block),
+            buffer(1, feed_block),
+            buffer(conv_block),
+            buffer(feed_block),
+            buffer(high - 1, conv_piece),
+            buffer(high - 1, feed_piece),
+            buffer(conv_rows),
+            buffer(feed_rows),
+            dma((2, seqs - 1)),
+            dma((2, seqs - 1)),
+            dma((4,)),
+            dma((4,)),
+            dma((2, high - 1)),
+            dma((2, high - 1)),
+            dma((2, high - 1)),
+            dma((2, high - 1)),
+            dma((4,)),
+            dma((4,)),
+        ],
+        compiler_params=pltpu.CompilerParams(
+            collective_id=0, has_side_effects=True, vmem_limit_bytes=40 * 2**20
+        ),
+    )(conv_pack, feed_pack)
+
+
+def padded_rows(value, parts):
+    unit = parts * 16
+    extra = -value.shape[1] % unit
+    return jnp.pad(value, ((0, 0), (0, extra), (0, 0)))
+
+
+def reduced(conv_term, embed_term, in_term, out_term):
+    seqs, dps = lax.axis_size("seq"), lax.axis_size("dp")
+    taps, chans = conv_term.shape[0], conv_term.shape[1]
+    part = chans // seqs
+    hidden = in_term.shape[1]
+    low = jnp.bfloat16
+    conv_pack = conv_term.astype(low).reshape(taps, seqs, part, chans)
+    conv_pack = conv_pack.transpose(1, 0, 2, 3).reshape(seqs, taps * part, chans)
+    kinds = taps * BASES
+    embed_pack = embed_term.astype(low).reshape(kinds, seqs, part).transpose(1, 0, 2)
+    embed_pack = jnp.pad(embed_pack, ((0, 0), (0, 0), (0, chans - part)))
+    conv_pack = padded_rows(jnp.concatenate([conv_pack, embed_pack], axis=1), 2 * dps)
+    feed_pack = jnp.concatenate(
+        [in_term.astype(low).reshape(seqs, part, hidden), out_term.astype(low).reshape(seqs, part, hidden)],
+        axis=1,
+    )
+    feed_pack = padded_rows(feed_pack, dps)
+    conv_sum, feed_sum = summed(conv_pack, feed_pack)
+    grad_conv = conv_sum[: taps * part].reshape(taps, part, chans)
+    grad_embed = conv_sum[taps * part : taps * part + kinds, :part].reshape(taps, BASES, part)
+    return grad_embed, grad_conv, feed_sum[:part], feed_sum[part : 2 * part].T
 
 
 def local(bases, embed, conv_w, w_in, w_out, cotangent):
@@ -104,17 +373,12 @@
         (partial_value[:half] + partner_sums(partial_value[half:])).astype(jnp.bfloat16)
     )
     dmixed_both = jnp.concatenate([dmixed, partner_rows(dmixed)], axis=0)
-    out_term = contract_rows(act, dmixed_both)
+    out_term = contract_rows(dmixed_both, act)
     dact = contract_cols(dmixed_both, out_cols)
     dpre = gelu_back(pre, dact).astype(jnp.bfloat16)
     in_term = contract_rows(both, dpre)
     dnormed_part = contract_cols(dpre, in_rows)
     dnormed = dnormed_part[:half] + partner_sums(dnormed_part[half:])
-    in_share, out_share = (
-        lax.psum_scatter(in_term, "seq", scatter_dimension=0, tiled=True),
-        lax.psum_scatter(out_term, "seq", scatter_dimension=1, tiled=True),
-    )
-    grad_in, grad_out = lax.psum((in_share, out_share), "dp")
     output = (h_onef + jnp.repeat(mixed.astype(jnp.float32), 2, axis=0)).astype(jnp.bfloat16)
     dpooled = scale * dnormed - pooledf * scale**3 * jnp.mean(
         dnormed * pooledf, axis=-1, keepdims=True
@@ -138,11 +402,7 @@
             for k in range(TAPS)
         ]
     )
-    conv_share, embed_share = (
-        lax.psum_scatter(conv_term, "seq", scatter_dimension=1, tiled=True),
-        lax.psum_scatter(embed_term, "seq", scatter_dimension=2, tiled=True),
-    )
-    grad_conv, grad_embed = lax.psum((conv_share, embed_share), ("dp", "sect"))
+    grad_embed, grad_conv, grad_in, grad_out = reduced(conv_term, embed_term, in_term, out_term)
     return (output[None], grad_embed, grad_conv, grad_in, grad_out)
 
 

time: 294 us -> 119 us (0.40)
  waiting for transfers between devices: 147 us -> 4.83 us
  blocking collectives: 81.6 us -> 4.01 us
  Pallas kernels: 0 us -> 47.7 us
  matrix products: 19.5 us -> 13.5 us
    psum x2 -> x0, waiting for transfers between devices: 120 us -> none  [the longest x1 120 us: local(): grad_conv, grad_embed = lax.psum((conv_share, embed_share), ('dp', 'sect'))]
    psum x1 -> x0, blocking collectives: 77.2 us -> none  [local(): grad_conv, grad_embed = lax.psum((conv_share, embed_share), ('dp', 'sect'))]
    pallas_call x0 -> x1, Pallas kernels: none -> 47.7 us  [summed(): pl.pallas_call(functools.partial(reduce_kernel, seqs, high), out_shape=(j...]
    reduce_scatter x3 -> x0, waiting for transfers between devices: 9.75 us -> none  [the longest x1 9.71 us: local(): lax.psum_scatter(conv_term, 'seq', scatter_dimension=1, tiled=True)]
    unnamed x49 -> x26, local copies, waits for them, and re-layouts: 8.22 us -> 1.38 us
    unnamed x8 -> x1, waiting for transfers between devices: 6.23 us -> 0.02 us
    dot_general x7, matrix products: 7.92 us -> 2.83 us  [contract_rows(): lax.dot_general(left, right, (((0,), (0,)), ((), ())), preferred_element_...]
    ppermute x4, waiting for transfers between devices: 7.45 us -> 3.34 us  [swapped(): return lax.ppermute(value, axis, pairs)]
  transfers between devices with their start and end apart: 17 -> 11, of which waited for: 10 -> 2; matrix products, arithmetic and copies ran while one was open for 8% -> 13% of each run, Pallas kernels for 0% -> 0%
where the time goes in v1:
time: 119 us; the launch traced here: 117 us
  Pallas kernels  47.7 us (40%)
  starting transfers between devices  18.5 us (16%)
  between operations  14.6 us (12%)
  matrix products  13.5 us (11%)
  local copies, waits for them, and re-layouts  8.28 us (7%)
  other arithmetic  5.42 us (5%)
  waiting for transfers between devices  4.83 us (4%)
  blocking collectives  4.01 us (3%)
    pallas_call x1, Pallas kernels, summed(): pl.pallas_call(functools.partial(reduce_kernel, seqs, high), out_shape=(j...  47.7 us
    ppermute x3, starting transfers between devices, padded(): lax.ppermute(tail, axis, [(i, (i + 1) % count) for i in range(ends)])  7.46 us
    ppermute x4, starting transfers between devices, swapped(): return lax.ppermute(value, axis, pairs)  6.99 us
    dot_general x5, matrix products, local(): jnp.dot(h_padded[k:k + rows], conv_full[k], preferred_element_type=jnp.fl...  4.24 us
    ppermute x3, starting transfers between devices, padded(): lax.ppermute(head, axis, [((i + 1) % count, i) for i in range(ends)])  4.04 us
    ppermute x4, waiting for transfers between devices, swapped(): return lax.ppermute(value, axis, pairs)  3.34 us
    dot_general x7, matrix products, contract_rows(): lax.dot_general(left, right, (((0,), (0,)), ((), ())), preferred_element_...  2.83 us
  transfers between devices with their start and end apart: 11, of which 2 were waited for; matrix products, arithmetic and copies ran while one was open for 13% of the time, Pallas kernels for 0%

profile of v1, /device:TPU:0, one launch (start us, length us, event | category | flops | bytes accessed | tf_op | source)
XLA Modules:
  0.0 116.8 jit_solution(14696869604056606052)
XLA Ops:
  7.2 0.7 broadcast_add_fusion
  8.0 1.3 %collective-permute-start.1 = (s32[2]{0:T(128)S(1)}, s32[2]{0:T(128)S(1)}, u32[]{:S(2)}, u32[]{:S(2)}) collective-permute-start(s32[2]{0:T(128)S(1)} %get-tuple-element.21), channel_id=1, source_target_pairs={{2,0},{3,1},{6,4},{7,5},{10,8},{11,9},{14,12},{15,13},{18,16},{19,... | collective-permute-start | bytes 32 | tf_op jit(solution)/shard_map/ppermute | solution.py:30
  9.3 3.0 %collective-permute-start = (s32[2]{0:T(128)S(1)}, s32[2]{0:T(128)S(1)}, u32[]{:S(2)}, u32[]{:S(2)}) collective-permute-start(s32[2]{0:T(128)S(1)} %get-tuple-element.22), channel_id=1, source_target_pairs={{0,2},{1,3},{4,6},{5,7},{8,10},{9,11},{12,14},{13,15},{16,18},{17,... | collective-permute-start | bytes 32 | tf_op jit(solution)/shard_map/ppermute | solution.py:28
  12.3 1.0 squeeze.49
  13.3 0.5 reduce_sum.41
  13.8 3.0 %collective-permute-start.6 = (bf16[128,384]{1,0:T(8,128)(2,1)S(1)}, bf16[128,384]{1,0:T(8,128)(2,1)S(1)}, u32[]{:S(2)}, u32[]{:S(2)}) collective-permute-start(bf16[128,384]{1,0:T(8,128)(2,1)S(1)} %reduce_sum.41), channel_id=1, source_target_pairs={{0,1},{1,0},{2,3},{3,2},{4,5},{5,4},{6,7},{7,6},{8,9},{9,8},{10,11... | collective-permute-start | bytes 294920 | tf_op jit(solution)/shard_map/ppermute | solution.py:17
  17.0 0.9 fusion.63
  18.0 0.3 convolution_add_fusion.7
  18.2 0.3 convolution_add_fusion.6
  18.5 0.3 convolution_add_fusion.5
  18.8 0.3 fusion.7
  19.0 1.3 %collective-permute-start.3 = (bf16[2,384]{1,0:T(2,128)(2,1)S(1)}, bf16[2,384]{1,0:T(2,128)(2,1)S(1)}, u32[]{:S(2)}, u32[]{:S(2)}) collective-permute-start(bf16[2,384]{1,0:T(2,128)(2,1)S(1)} %get-tuple-element.14), channel_id=1, source_target_pairs={{2,0},{3,1},{6,4},{7,5},{10,8},{11,9},{14,12},{15,13},{18,16},{19,... | collective-permute-start | bytes 4616 | tf_op jit(solution)/shard_map/ppermute | solution.py:30
  20.3 3.0 %collective-permute-start.2 = (bf16[2,384]{1,0:T(2,128)(2,1)S(1)}, bf16[2,384]{1,0:T(2,128)(2,1)S(1)}, u32[]{:S(2)}, u32[]{:S(2)}) collective-permute-start(bf16[2,384]{1,0:T(2,128)(2,1)S(1)} %get-tuple-element.13), channel_id=1, source_target_pairs={{0,2},{1,3},{4,6},{5,7},{8,10},{9,11},{12,14},{13,15},{16,18},{17,... | collective-permute-start | bytes 4616 | tf_op jit(solution)/shard_map/ppermute | solution.py:28
  23.4 1.5 %all-gather.2.cloned.1.call-done = bf16[5,384,384]{2,1,0:T(8,128)(2,1)} async-done(((bf16[5,192,384]{2,1,0:T(8,128)(2,1)}), bf16[5,384,384]{2,1,0:T(8,128)(2,1)}) %all-gather.2.cloned.1.call-update) | async-done | bytes 1474576 | tf_op jit(solution)/shard_map/all_gather | solution.py:345
  24.8 1.3 %fusion.35 = f32[256,384]{1,0:T(8,128)S(1)} fusion(bf16[256,384]{1,0:T(8,128)(2,1)S(1)} %fusion.7, bf16[5,384,384]{2,1,0:T(8,128)(2,1)} %all-gather.2.cloned.1.call-done), kind=kOutput, calls=%fused_computation.75 | convolution fusion | flops 75497472 | bytes 884736 | tf_op jit(solution)/shard_map/dot_general | solution.py:349
  26.2 1.2 %fusion.37 = f32[256,384]{1,0:T(8,128)S(1)} fusion(bf16[5,384,384]{2,1,0:T(8,128)(2,1)} %all-gather.2.cloned.1.call-done, bf16[2,384]{1,0:T(2,128)(2,1)S(1)} %collective-permute-done.3, bf16[256,384]{1,0:T(8,128)(2,1)S(1)} %fusion.7), kind=kOutput, calls=%fused_computation.77 | convolution fusion | flops 75890688 | bytes 886272 | tf_op jit(solution)/shard_map/dot_general | solution.py:349
  27.5 0.3 fusion.33
  27.7 0.3 fusion.2
  28.0 1.1 add_convert_fusion.1
  29.2 0.7 copy-done.5
  29.8 0.2 reshape.92
  30.0 0.5 reduce_sum.39
  30.8 1.8 %collective-permute-start.4 = (bf16[128,384]{1,0:T(8,128)(2,1)S(1)}, bf16[128,384]{1,0:T(8,128)(2,1)S(1)}, u32[]{:S(2)}, u32[]{:S(2)}) collective-permute-start(bf16[128,384]{1,0:T(8,128)(2,1)S(1)} %fusion.45), channel_id=1, source_target_pairs={{0,1},{1,0},{2,3},{3,2},{4,5},{5,4},{6,7},{7,6},{8,9},{9,8},{10,11... | collective-permute-start | bytes 294920 | tf_op jit(solution)/shard_map/ppermute | solution.py:17
  32.5 2.0 %all_gather.11 = bf16[384,384]{0,1:T(8,128)(2,1)S(1)} all-gather(bf16[384,192]{0,1:T(8,128)(2,1)S(1)} %copy-done.8), channel_id=1, replica_groups=mesh['dp'=8,'seq'=2,'sect'=2] {'seq'}, dimensions={1}, use_global_device_ids=true | all-gather | bytes 442368 | tf_op jit(solution)/shard_map/all_gather | solution.py:364
  34.6 2.0 %all_gather.10 = bf16[384,384]{1,0:T(8,128)(2,1)S(1)} all-gather(bf16[192,384]{1,0:T(8,128)(2,1)S(1)} %copy-done.9), channel_id=1, replica_groups=mesh['dp'=8,'seq'=2,'sect'=2] {'seq'}, dimensions={0}, use_global_device_ids=true | all-gather | bytes 442368 | tf_op jit(solution)/shard_map/all_gather | solution.py:363
  36.6 0.3 fusion.66
  36.8 0.3 fusion.113
  37.2 1.0 collective-permute-start.5
  38.2 0.4 fusion.31
  38.7 0.3 fusion.118
  39.0 1.1 collective-permute-start.7
  40.1 0.4 convolution_convert_fusion
  40.5 0.3 convolution_convert_fusion.1
  40.9 3.3 %collective-permute-done.7 = bf16[128,384]{1,0:T(8,128)(2,1)S(1)} collective-permute-done((bf16[128,384]{1,0:T(8,128)(2,1)S(1)}, bf16[128,384]{1,0:T(8,128)(2,1)S(1)}, u32[]{:S(2)}, u32[]{:S(2)}) %collective-permute-start.7) | collective-permute-done | bytes 98336 | tf_op jit(solution)/shard_map/ppermute | solution.py:17
  44.5 0.1 broadcast_in_dim.8
  44.6 0.3 reshape.94
  44.9 1.3 %fusion.24 = bf16[256,384]{1,0:T(8,128)(2,1)S(1)} fusion(f32[256,384]{1,0:T(8,128)} %get-tuple-element.26, f32[256,384]{1,0:T(8,128)S(1)} %reshape.94, bf16[1,256,384]{2,1,0:T(8,128)(2,1)S(1)} %copy-done.3), kind=kLoop, calls=%fused_computation.50 | loop fusion | flops 2162688 | bytes 1179648 | tf_op jit(solution)/shard_map/convert_element_type | solution.py:387
  46.2 1.0 convolution_convert_fusion.4
  47.3 0.8 broadcast_in_dim.6
  48.2 1.3 %reshape.93 = f32[256,384]{1,0:T(8,128)S(1)} reshape(f32[128,2,384]{2,1,0:T(2,128)} %broadcast_in_dim.6) | data formatting | bytes 786432 | tf_op jit(solution)/shard_map/reshape | solution.py:382
  49.4 1.6 %fusion.50 = bf16[1,256,384]{2,1,0:T(8,128)(2,1)} fusion(f32[256,384]{1,0:T(8,128)S(1)} %reshape.93, bf16[256,384]{1,0:T(8,128)(2,1)} %copy-done.5), kind=kLoop, calls=%fused_computation.96 | loop fusion | flops 294912 | bytes 786432 | tf_op jit(solution)/shard_map/broadcast_in_dim | solution.py:406
  51.1 1.4 %collective-permute-start.9 = (bf16[2,384]{1,0:T(2,128)(2,1)S(1)}, bf16[2,384]{1,0:T(2,128)(2,1)S(1)}, u32[]{:S(2)}, u32[]{:S(2)}) collective-permute-start(bf16[2,384]{1,0:T(2,128)(2,1)S(1)} %get-tuple-element.12), channel_id=1, source_target_pairs={{0,2},{1,3},{4,6},{5,7},{8,10},{9,11},{12,14},{13,15},{16,18},{17,... | collective-permute-start | bytes 4616 | tf_op jit(solution)/shard_map/ppermute | solution.py:28
  52.5 1.5 %collective-permute-start.8 = (bf16[2,384]{1,0:T(2,128)(2,1)S(1)}, bf16[2,384]{1,0:T(2,128)(2,1)S(1)}, u32[]{:S(2)}, u32[]{:S(2)}) collective-permute-start(bf16[2,384]{1,0:T(2,128)(2,1)S(1)} %get-tuple-element.11), channel_id=1, source_target_pairs={{2,0},{3,1},{6,4},{7,5},{10,8},{11,9},{14,12},{15,13},{18,16},{19,... | collective-permute-start | bytes 4616 | tf_op jit(solution)/shard_map/ppermute | solution.py:30
  54.0 0.3 convolution_convert_fusion.6
  54.3 0.3 convolution_convert_fusion.5
  54.7 0.3 convolution_convert_fusion.3
  55.1 0.3 fusion.34
  55.4 0.3 convolution_convert_fusion.2
  55.8 0.3 fusion.36
  56.1 0.3 fusion.32
  56.4 0.5 copy-done.1
  56.8 0.3 fusion.5
  57.2 0.3 fusion.6
  57.5 0.3 fusion.9
  57.8 0.3 fusion.11
  58.1 0.3 fusion.13
  58.5 0.3 fusion.15
  58.8 0.3 fusion.17
  59.3 0.2 fusion.1
  59.4 0.2 pad.9.conv_in
  59.6 47.7 %shard_map.101 = (f32[1024,384]{1,0:T(8,128)S(1)}, f32[384,384]{1,0:T(8,128)S(1)}) custom-call(bf16[2,1024,384]{2,1,0:T(8,128)(2,1)S(1)} %pad.9.conv_in, bf16[2,384,384]{2,1,0:T(8,128)(2,1)S(1)} %pad_maximum_fusion.feed_in), custom_call_target="tpu_custom_call" | custom-call | tf_op jit(solution)/shard_map/pallas_call | solution.py:264
  107.3 1.2 %slice.172 = f32[960,384]{1,0:T(8,128)} slice(f32[1024,384]{1,0:T(8,128)S(1)} %get-tuple-element.7), slice={[0:960], [0:384]} | slice | bytes 2949120 | tf_op jit(solution)/shard_map/slice | solution.py:326
  108.5 0.6 reshape.98
  109.1 0.8 slice_bitcast_fusion.5
  (56 shorter events, 1.3 us)
Async XLA Ops:
  7.2 10.8 %copy-start.10 = (bf16[5,4,384]{2,1,0:T(4,128)(2,1)S(1)}, bf16[5,4,384]{2,1,0:T(4,128)(2,1)}, u32[]{:S(2)}) copy-start(bf16[5,4,384]{2,1,0:T(4,128)(2,1)} %param.7) | copy-start | bytes 46084
  7.2 17.7 %all-gather.2.cloned.1.call-start = ((), (), s32[]{:S(2)}) async-start(), calls=%async_computation | async-start | bytes 2211840 | tf_op jit(solution)/shard_map/all_gather | solution.py:345
  8.0 8.9 %collective-permute-start.1 = (s32[2]{0:T(128)S(1)}, s32[2]{0:T(128)S(1)}, u32[]{:S(2)}, u32[]{:S(2)}) collective-permute-start(s32[2]{0:T(128)S(1)} %get-tuple-element.21), channel_id=1, source_target_pairs={{2,0},{3,1},{6,4},{7,5},{10,8},{11,9},{14,12},{15,13},{18,16},{19,... | collective-permute-start | bytes 32 | tf_op jit(solution)/shard_map/ppermute | solution.py:30
  9.3 7.6 %collective-permute-start = (s32[2]{0:T(128)S(1)}, s32[2]{0:T(128)S(1)}, u32[]{:S(2)}, u32[]{:S(2)}) collective-permute-start(s32[2]{0:T(128)S(1)} %get-tuple-element.22), channel_id=1, source_target_pairs={{0,2},{1,3},{4,6},{5,7},{8,10},{9,11},{12,14},{13,15},{16,18},{17,... | collective-permute-start | bytes 32 | tf_op jit(solution)/shard_map/ppermute | solution.py:28
  13.8 24.4 %collective-permute-start.6 = (bf16[128,384]{1,0:T(8,128)(2,1)S(1)}, bf16[128,384]{1,0:T(8,128)(2,1)S(1)}, u32[]{:S(2)}, u32[]{:S(2)}) collective-permute-start(bf16[128,384]{1,0:T(8,128)(2,1)S(1)} %reduce_sum.41), channel_id=1, source_target_pairs={{0,1},{1,0},{2,3},{3,2},{4,5},{5,4},{6,7},{7,6},{8,9},{9,8},{10,11... | collective-permute-start | bytes 294920 | tf_op jit(solution)/shard_map/ppermute | solution.py:17
  19.0 7.1 %collective-permute-start.3 = (bf16[2,384]{1,0:T(2,128)(2,1)S(1)}, bf16[2,384]{1,0:T(2,128)(2,1)S(1)}, u32[]{:S(2)}, u32[]{:S(2)}) collective-permute-start(bf16[2,384]{1,0:T(2,128)(2,1)S(1)} %get-tuple-element.14), channel_id=1, source_target_pairs={{2,0},{3,1},{6,4},{7,5},{10,8},{11,9},{14,12},{15,13},{18,16},{19,... | collective-permute-start | bytes 4616 | tf_op jit(solution)/shard_map/ppermute | solution.py:30
  20.3 7.1 %collective-permute-start.2 = (bf16[2,384]{1,0:T(2,128)(2,1)S(1)}, bf16[2,384]{1,0:T(2,128)(2,1)S(1)}, u32[]{:S(2)}, u32[]{:S(2)}) collective-permute-start(bf16[2,384]{1,0:T(2,128)(2,1)S(1)} %get-tuple-element.13), channel_id=1, source_target_pairs={{0,2},{1,3},{4,6},{5,7},{8,10},{9,11},{12,14},{13,15},{16,18},{17,... | collective-permute-start | bytes 4616 | tf_op jit(solution)/shard_map/ppermute | solution.py:28
  24.8 2.6 %copy-start = (bf16[5,384,384]{2,1,0:T(8,128)(2,1)S(1)}, bf16[5,384,384]{2,1,0:T(8,128)(2,1)}, u32[]{:S(2)}) copy-start(bf16[5,384,384]{2,1,0:T(8,128)(2,1)} %all-gather.2.cloned.1.call-done) | copy-start | bytes 4423684
  28.0 4.5 %copy-start.8 = (bf16[384,192]{0,1:T(8,128)(2,1)S(1)}, bf16[384,192]{0,1:T(8,128)(2,1)}, u32[]{:S(2)}) copy-start(bf16[384,192]{0,1:T(8,128)(2,1)} %param.10) | copy-start | bytes 442372
  29.2 0.7 copy-start.5
  29.2 5.4 %copy-start.9 = (bf16[192,384]{1,0:T(8,128)(2,1)S(1)}, bf16[192,384]{1,0:T(8,128)(2,1)}, u32[]{:S(2)}) copy-start(bf16[192,384]{1,0:T(8,128)(2,1)} %param.9) | copy-start | bytes 442372
  30.8 5.8 %collective-permute-start.4 = (bf16[128,384]{1,0:T(8,128)(2,1)S(1)}, bf16[128,384]{1,0:T(8,128)(2,1)S(1)}, u32[]{:S(2)}, u32[]{:S(2)}) collective-permute-start(bf16[128,384]{1,0:T(8,128)(2,1)S(1)} %fusion.45), channel_id=1, source_target_pairs={{0,1},{1,0},{2,3},{3,2},{4,5},{5,4},{6,7},{7,6},{8,9},{9,8},{10,11... | collective-permute-start | bytes 294920 | tf_op jit(solution)/shard_map/ppermute | solution.py:17
  37.2 1.8 %copy-start.6 = (f32[256,384]{1,0:T(8,128)}, f32[256,384]{1,0:T(8,128)S(1)}, u32[]{:S(2)}) copy-start(f32[256,384]{1,0:T(8,128)S(1)} %fusion.113) | copy-start | bytes 1179652
  37.2 10.1 %collective-permute-start.5 = (bf16[128,384]{1,0:T(8,128)(2,1)S(1)}, bf16[128,384]{1,0:T(8,128)(2,1)S(1)}, u32[]{:S(2)}, u32[]{:S(2)}) collective-permute-start(bf16[128,384]{1,0:T(8,128)(2,1)S(1)} %slice.283), channel_id=1, source_target_pairs={{0,1},{1,0},{2,3},{3,2},{4,5},{5,4},{6,7},{7,6},{8,9},{9,8},{10,11... | collective-permute-start | bytes 294920 | tf_op jit(solution)/shard_map/ppermute | solution.py:17
  39.0 5.2 %collective-permute-start.7 = (bf16[128,384]{1,0:T(8,128)(2,1)S(1)}, bf16[128,384]{1,0:T(8,128)(2,1)S(1)}, u32[]{:S(2)}, u32[]{:S(2)}) collective-permute-start(bf16[128,384]{1,0:T(8,128)(2,1)S(1)} %slice.282), channel_id=1, source_target_pairs={{0,1},{1,0},{2,3},{3,2},{4,5},{5,4},{6,7},{7,6},{8,9},{9,8},{10,11... | collective-permute-start | bytes 294920 | tf_op jit(solution)/shard_map/ppermute | solution.py:17
  40.9 4.0 %copy-start.3 = (bf16[1,256,384]{2,1,0:T(8,128)(2,1)S(1)}, bf16[1,256,384]{2,1,0:T(8,128)(2,1)}, u32[]{:S(2)}) copy-start(bf16[1,256,384]{2,1,0:T(8,128)(2,1)} %param.11) | copy-start | bytes 589828
  44.9 2.4 %copy-start.7 = (f32[256,384]{1,0:T(8,128)S(1)}, f32[256,384]{1,0:T(8,128)}, u32[]{:S(2)}) copy-start(f32[256,384]{1,0:T(8,128)} %copy-done.6) | copy-start | bytes 1179652
  51.1 3.6 %copy-start.4 = (bf16[384,384]{1,0:T(8,128)(2,1)S(1)}, bf16[384,384]{1,0:T(8,128)(2,1)}, u32[]{:S(2)}) copy-start(bf16[384,384]{1,0:T(8,128)(2,1)} %convolution_convert_fusion.4) | copy-start | bytes 884740
  51.1 4.7 %collective-permute-start.9 = (bf16[2,384]{1,0:T(2,128)(2,1)S(1)}, bf16[2,384]{1,0:T(2,128)(2,1)S(1)}, u32[]{:S(2)}, u32[]{:S(2)}) collective-permute-start(bf16[2,384]{1,0:T(2,128)(2,1)S(1)} %get-tuple-element.12), channel_id=1, source_target_pairs={{0,2},{1,3},{4,6},{5,7},{8,10},{9,11},{12,14},{13,15},{16,18},{17,... | collective-permute-start | bytes 4616 | tf_op jit(solution)/shard_map/ppermute | solution.py:28
  52.5 3.6 %collective-permute-start.8 = (bf16[2,384]{1,0:T(2,128)(2,1)S(1)}, bf16[2,384]{1,0:T(2,128)(2,1)S(1)}, u32[]{:S(2)}, u32[]{:S(2)}) collective-permute-start(bf16[2,384]{1,0:T(2,128)(2,1)S(1)} %get-tuple-element.11), channel_id=1, source_target_pairs={{2,0},{3,1},{6,4},{7,5},{10,8},{11,9},{14,12},{15,13},{18,16},{19,... | collective-permute-start | bytes 4616 | tf_op jit(solution)/shard_map/ppermute | solution.py:30
  55.7 1.1 copy-start.1
  57.5 1.8 %copy-start.2 = (bf16[5,2,192,384]{3,2,0,1:T(8,128)(2,1)S(1)}, bf16[5,2,192,384]{3,2,0,1:T(8,128)(2,1)}, u32[]{:S(2)}) copy-start(bf16[5,2,192,384]{3,2,0,1:T(8,128)(2,1)} %copy-done.1) | copy-start | bytes 4423684
Sparse Core Ops, SparseCore 0:
  12.4 12.3 all-gather.1

commit v2 on v1

--- a/solution.py
+++ b/solution.py
@@ -328,22 +328,104 @@
     return grad_embed, grad_conv, feed_sum[:part], feed_sum[part : 2 * part].T
 
 
+def gather_kernel(
+    seqs, conv_w, in_w, out_w, ids, dmixed, conv_full, in_full, out_full, ids_near, both,
+    send, recv, id_send, id_recv, row_send, row_recv,
+):
+    me = lax.axis_index("seq")
+    peers = [{"seq": lax.rem(me + k, seqs)} for k in range(1, seqs)]
+    partner = {"sect": 1 - lax.axis_index("sect")}
+    barrier = pltpu.get_barrier_semaphore()
+    for place in peers + [partner]:
+        pl.semaphore_signal(
+            barrier, inc=1, device_id=place, device_id_type=pl.DeviceIdType.MESH
+        )
+    pl.semaphore_wait(barrier, len(peers) + 1)
+    part, half = in_w.shape[0], dmixed.shape[0]
+    mine = pl.ds(pl.multiple_of(me * part, part), part)
+    copies = [
+        remote(ids, ids_near.at[0], id_send.at[0], id_recv.at[0], peers[0]),
+        remote(ids, ids_near.at[1], id_send.at[1], id_recv.at[1], peers[-1]),
+        remote(dmixed, both.at[pl.ds(half, half)], row_send, row_recv, partner),
+    ]
+    for k, place in enumerate(peers):
+        copies += [
+            remote(conv_w, conv_full.at[:, mine], send.at[0, k], recv.at[0, k], place),
+            remote(in_w, in_full.at[mine], send.at[1, k], recv.at[1, k], place),
+            remote(out_w, out_full.at[mine], send.at[2, k], recv.at[2, k], place),
+        ]
+    for copy in copies:
+        copy.start()
+    for tap in range(conv_w.shape[0]):
+        conv_full[tap, mine] = conv_w[tap]
+    in_full[mine] = in_w[...]
+    out_full[mine] = out_w[...]
+    both[pl.ds(0, half)] = dmixed[...]
+    for copy in copies:
+        copy.wait_recv()
+    for copy in copies:
+        copy.wait_send()
+
+
+def gathered(conv_w, in_w, out_w, ids, dmixed):
+    seqs = lax.axis_size("seq")
+    taps, part, chans = conv_w.shape
+    low = jnp.bfloat16
+    dma = pltpu.SemaphoreType.DMA
+    return pl.pallas_call(
+        functools.partial(gather_kernel, seqs),
+        out_shape=(
+            jax.ShapeDtypeStruct((taps, part * seqs, chans), low),
+            jax.ShapeDtypeStruct((part * seqs, in_w.shape[1]), low),
+            jax.ShapeDtypeStruct((part * seqs, out_w.shape[1]), low),
+            jax.ShapeDtypeStruct((2,) + ids.shape, jnp.int32),
+            jax.ShapeDtypeStruct((2 * dmixed.shape[0], chans), low),
+        ),
+        in_specs=[pl.BlockSpec(memory_space=pltpu.VMEM)] * 5,
+        out_specs=[pl.BlockSpec(memory_space=pltpu.VMEM)] * 5,
+        scratch_shapes=[
+            dma((3, seqs - 1)),
+            dma((3, seqs - 1)),
+            dma((2,)),
+            dma((2,)),
+            dma(()),
+            dma(()),
+        ],
+        compiler_params=pltpu.CompilerParams(
+            collective_id=1, has_side_effects=True, vmem_limit_bytes=32 * 2**20
+        ),
+    )(conv_w, in_w, out_w, ids, dmixed)
+
+
 def local(bases, embed, conv_w, w_in, w_out, cotangent):
     rows = bases.shape[1]
     chans = embed.shape[2]
     half = rows // 2
-    padded_ids = padded(bases[0] + 1, (("seq", 0),), 2)
+    seq, ends = lax.axis_index("seq"), lax.axis_size("seq") - 1
+    ids = bases + 1
+    dout = cotangent[0].astype(jnp.float32)
+    dmixed = dout.reshape(half, 2, chans).sum(1).astype(jnp.bfloat16)
+    conv_full, in_rows, out_rows, ids_near, dmixed_both = gathered(
+        conv_w, w_in, w_out.T, ids, dmixed
+    )
+    before = jnp.where(seq > 0, ids_near[0, 0, rows - 4 :], 0)
+    after = jnp.where(seq < ends, ids_near[1, 0, :4], 0)
+    padded_ids = jnp.concatenate([before, ids[0], after])
     levels = jnp.arange(1, BASES + 1, dtype=jnp.int32)
-    onehots = [
-        (padded_ids[k : k + rows, None] == levels[None, :]).astype(jnp.bfloat16)
-        for k in range(TAPS)
-    ]
-    accum = jnp.zeros((rows, chans), jnp.float32)
-    for k in range(TAPS):
-        accum = accum + jnp.dot(onehots[k], embed[k], preferred_element_type=jnp.float32)
-    h_zero = accum.astype(jnp.bfloat16)
-    conv_full = lax.all_gather(conv_w, "seq", axis=1, tiled=True)
-    h_padded = padded(h_zero, (("seq", 0),), 2)
+    wide_hots = jnp.concatenate(
+        [
+            (padded_ids[k : k + rows + 4, None] == levels[None, :]).astype(jnp.bfloat16)
+            for k in range(TAPS)
+        ],
+        axis=1,
+    )
+    accum = jnp.dot(
+        wide_hots, embed.reshape(TAPS * BASES, chans), preferred_element_type=jnp.float32
+    )
+    place = jnp.arange(rows + 4)[:, None]
+    inside = ((place >= 2) | (seq > 0)) & ((place < rows + 2) | (seq < ends))
+    h_padded = jnp.where(inside, accum, 0.0).astype(jnp.bfloat16)
+    h_zero = h_padded[2 : 2 + rows]
     pre_conv = jnp.zeros((rows, chans), jnp.float32)
     for k in range(TAPS):
         pre_conv = pre_conv + jnp.dot(
@@ -359,22 +441,15 @@
     pooledf = pooled.astype(jnp.float32)
     scale = lax.rsqrt(jnp.mean(pooledf * pooledf, axis=-1, keepdims=True) + 1e-06)
     normed = (pooledf * scale).astype(jnp.bfloat16)
-    in_rows, out_cols = (
-        lax.all_gather(w_in, "seq", axis=0, tiled=True),
-        lax.all_gather(w_out, "seq", axis=1, tiled=True),
-    )
-    dout = cotangent[0].astype(jnp.float32)
-    dmixed = dout.reshape(half, 2, chans).sum(1).astype(jnp.bfloat16)
     both = jnp.concatenate([normed, partner_rows(normed)], axis=0)
     pre = jnp.dot(both, in_rows, preferred_element_type=jnp.float32)
     act = gelu_tanh(pre).astype(jnp.bfloat16)
-    partial_value = jnp.dot(act, out_cols, preferred_element_type=jnp.float32)
+    partial_value = contract_cols(act, out_rows)
     mixed = lax.optimization_barrier(
         (partial_value[:half] + partner_sums(partial_value[half:])).astype(jnp.bfloat16)
     )
-    dmixed_both = jnp.concatenate([dmixed, partner_rows(dmixed)], axis=0)
     out_term = contract_rows(dmixed_both, act)
-    dact = contract_cols(dmixed_both, out_cols)
+    dact = jnp.dot(dmixed_both, out_rows, preferred_element_type=jnp.float32)
     dpre = gelu_back(pre, dact).astype(jnp.bfloat16)
     in_term = contract_rows(both, dpre)
     dnormed_part = contract_cols(dpre, in_rows)
@@ -390,17 +465,12 @@
     for k in range(TAPS):
         dh_zero = dh_zero + contract_cols(dz_padded[4 - k : 4 - k + rows], conv_full[k])
     conv_term = jnp.stack([contract_rows(h_padded[k : k + rows], dz_rows) for k in range(TAPS)])
-    embed_term = jnp.stack(
-        [
-            lax.dot_general(
-                onehots[k].astype(jnp.float32),
-                dh_zero,
-                (((0,), (0,)), ((), ())),
-                precision=lax.Precision.HIGHEST,
-                preferred_element_type=jnp.float32,
-            )
-            for k in range(TAPS)
-        ]
+    embed_term = lax.dot_general(
+        wide_hots[2 : 2 + rows].astype(jnp.float32),
+        dh_zero,
+        (((0,), (0,)), ((), ())),
+        precision=lax.Precision.HIGHEST,
+        preferred_element_type=jnp.float32,
     )
     grad_embed, grad_conv, grad_in, grad_out = reduced(conv_term, embed_term, in_term, out_term)
     return (output[None], grad_embed, grad_conv, grad_in, grad_out)

time: 119 us -> 102 us (0.86)
  between operations: 14.6 us -> 1.14 us
  starting transfers between devices: 18.5 us -> 5.94 us
  Pallas kernels: 47.7 us -> 54.4 us
  local copies, waits for them, and re-layouts: 8.28 us -> 12.4 us
  blocking collectives: 4.01 us -> 0 us
  other arithmetic: 5.42 us -> 8.12 us
  matrix products: 13.5 us -> 11.4 us
  waiting for transfers between devices: 4.83 us -> 6.72 us
    pallas_call x0 -> x1, Pallas kernels: none -> 6.55 us  [gathered(): pl.pallas_call(functools.partial(gather_kernel, seqs), out_shape=(jax.Sha...]
    ppermute x3 -> x1, starting transfers between devices: 7.46 us -> 1.28 us  [padded(): lax.ppermute(tail, axis, [(i, (i + 1) % count) for i in range(ends)])]
    all_gather x2 -> x0, blocking collectives: 4.01 us -> none  [the longest x1 2.01 us: local(): lax.all_gather(w_in, 'seq', axis=0, tiled=True)]
    ppermute x4 -> x3, starting transfers between devices: 6.99 us -> 3.37 us  [swapped(): return lax.ppermute(value, axis, pairs)]
    unnamed x26 -> x36, local copies, waits for them, and re-layouts: 1.38 us -> 4.84 us
    ppermute x4 -> x3, waiting for transfers between devices: 3.34 us -> 6.56 us  [swapped(): return lax.ppermute(value, axis, pairs)]
    dot_general x11 -> x3, matrix products: 3.91 us -> 0.8 us  [the longest x1 0.27 us: local(): jnp.dot(wide_hots, embed.reshape(TAPS * BASES, chans), preferred_element_...]
    dot_general x7, matrix products: 2.83 us -> 5.75 us  [contract_rows(): lax.dot_general(left, right, (((0,), (0,)), ((), ())), preferred_element_...]
  transfers between devices with their start and end apart: 11 -> 5, of which waited for: 2 -> 3; matrix products, arithmetic and copies ran while one was open for 13% -> 10% of each run, Pallas kernels for 0% -> 0%
where the time goes in v2:
time: 102 us; the launch traced here: 100 us
  Pallas kernels  54.4 us (53%)
  local copies, waits for them, and re-layouts  12.4 us (12%)
  matrix products  11.4 us (11%)
  other arithmetic  8.12 us (8%)
  waiting for transfers between devices  6.72 us (7%)
  starting transfers between devices  5.94 us (6%)
  between operations  1.14 us (1%)
    pallas_call x1, Pallas kernels, summed(): pl.pallas_call(functools.partial(reduce_kernel, seqs, high), out_shape=(j...  47.9 us
    ppermute x3, waiting for transfers between devices, swapped(): return lax.ppermute(value, axis, pairs)  6.56 us
    pallas_call x1, Pallas kernels, gathered(): pl.pallas_call(functools.partial(gather_kernel, seqs), out_shape=(jax.Sha...  6.55 us
    dot_general x7, matrix products, contract_rows(): lax.dot_general(left, right, (((0,), (0,)), ((), ())), preferred_element_...  5.75 us
    unnamed x36, local copies, waits for them, and re-layouts  4.84 us
    ppermute x3, starting transfers between devices, swapped(): return lax.ppermute(value, axis, pairs)  3.37 us
    dot_general x5, matrix products, local(): jnp.dot(h_padded[k:k + rows], conv_full[k], preferred_element_type=jnp.fl...  2.23 us
    dot_general x7, matrix products, contract_cols(): lax.dot_general(left, right, (((1,), (1,)), ((), ())), preferred_element_...  2.1 us
  transfers between devices with their start and end apart: 5, of which 3 were waited for; matrix products, arithmetic and copies ran while one was open for 10% of the time, Pallas kernels for 0%

profile of v2, /device:TPU:0, one launch (start us, length us, event | category | flops | bytes accessed | tf_op | source)
XLA Modules:
  0.0 100.1 jit_solution(11146080830329071862)
XLA Ops:
  0.7 0.7 broadcast_add_fusion.ids
  1.3 1.0 squeeze.28
  2.4 0.5 reduce_sum.39.dmixed
  2.9 1.1 %copy-done = bf16[5,192,384]{2,1,0:T(8,128)(2,1)S(1)} copy-done((bf16[5,192,384]{2,1,0:T(8,128)(2,1)S(1)}, bf16[5,192,384]{2,1,0:T(8,128)(2,1)}, u32[]{:S(2)}) %copy-start) | copy-done | bytes 737304
  4.0 0.9 copy-done.1
  4.9 0.9 copy-done.2
  5.8 6.6 %shard_map.101 = (bf16[5,384,384]{2,1,0:T(8,128)(2,1)S(1)}, bf16[384,384]{1,0:T(8,128)(2,1)S(1)}, bf16[384,384]{1,0:T(8,128)(2,1)S(1)}, s32[2,1,256]{2,1,0:T(1,128)S(1)}, bf16[256,384]{1,0:T(8,128)(2,1)S(1)}) custom-call(bf16[5,192,384]{2,1,0:T(8,128)(2,1)S(1)} %copy-done, bf16[192,384]{1,0:T(8,128)(2,1)S(1)} %copy-done.1, bf16[192,384]{1,0:T(8,128)(2,1)S(1)} %bitcast.82, ...), custom_call_target="tpu_custom_call" | custom-call | tf_op jit(solution)/shard_map/pallas_call | solution.py:375
  12.4 0.1 pad_add_fusion.1
  12.5 0.1 pad_add_fusion.2
  12.6 0.1 broadcast_compare_fusion
  12.7 0.1 concatenate.38
  12.8 0.3 fusion.5
  13.1 0.3 fusion.32
  13.4 0.3 convolution_add_fusion.5
  13.6 0.3 convolution_add_fusion.4
  13.9 0.3 convolution_add_fusion.3
  14.2 1.1 %add_convert_fusion.1 = (bf16[256,384]{1,0:T(8,128)(2,1)S(1)}, f32[256,384]{1,0:T(8,128)}) fusion(bf16[260,384]{1,0:T(8,128)(2,1)S(1)} %fusion.5, f32[256,384]{1,0:T(8,128)S(1)} %convolution_add_fusion.3, bf16[5,384,384]{2,1,0:T(8,128)(2,1)S(1)} %get-tuple-element.13), kind=kOutput, calls=%fused_computation.44 | convolution fusion | flops 76677120 | bytes 1671168 | tf_op jit(solution)/shard_map/dot_general | solution.py:431
  15.4 0.7 copy-done.5
  16.0 0.2 reshape.109
  16.2 0.5 reduce_sum.40
  16.7 0.1 fusion.48
  16.9 0.1 fusion.49
  17.0 1.2 %collective-permute-start = (bf16[128,384]{1,0:T(8,128)(2,1)S(1)}, bf16[128,384]{1,0:T(8,128)(2,1)S(1)}, u32[]{:S(2)}, u32[]{:S(2)}) collective-permute-start(bf16[128,384]{1,0:T(8,128)(2,1)S(1)} %fusion.49), channel_id=1, source_target_pairs={{0,1},{1,0},{2,3},{3,2},{4,5},{5,4},{6,7},{7,6},{8,9},{9,8},{10,11... | collective-permute-start | bytes 294920 | tf_op jit(solution)/shard_map/ppermute | solution.py:17
  18.2 0.3 fusion.84
  18.4 3.2 %collective-permute-done = bf16[128,384]{1,0:T(8,128)(2,1)S(1)} collective-permute-done((bf16[128,384]{1,0:T(8,128)(2,1)S(1)}, bf16[128,384]{1,0:T(8,128)(2,1)S(1)}, u32[]{:S(2)}, u32[]{:S(2)}) %collective-permute-start) | collective-permute-done | bytes 98336 | tf_op jit(solution)/shard_map/ppermute | solution.py:17
  21.6 0.5 fusion.19
  22.1 0.3 fusion.81
  22.5 0.4 convolution_convert_fusion
  22.9 1.2 %collective-permute-start.1 = (bf16[128,384]{1,0:T(8,128)(2,1)S(1)}, bf16[128,384]{1,0:T(8,128)(2,1)}, u32[]{:S(2)}, u32[]{:S(2)}) collective-permute-start(bf16[128,384]{1,0:T(8,128)(2,1)S(1)} %slice.247), channel_id=1, source_target_pairs={{0,1},{1,0},{2,3},{3,2},{4,5},{5,4},{6,7},{7,6},{8,9},{9,8},{10,11... | collective-permute-start | bytes 294920 | tf_op jit(solution)/shard_map/ppermute | solution.py:17
  24.1 0.3 fusion.85
  24.4 1.0 collective-permute-start.2
  25.3 0.3 convolution_convert_fusion.1
  25.7 3.4 %collective-permute-done.2 = bf16[128,384]{1,0:T(8,128)(2,1)S(1)} collective-permute-done((bf16[128,384]{1,0:T(8,128)(2,1)S(1)}, bf16[128,384]{1,0:T(8,128)(2,1)S(1)}, u32[]{:S(2)}, u32[]{:S(2)}) %collective-permute-start.2) | collective-permute-done | bytes 98336 | tf_op jit(solution)/shard_map/ppermute | solution.py:17
  29.1 0.1 fusion.53
  29.2 0.1 fusion.52
  29.3 0.1 broadcast_in_dim.44
  29.5 0.3 reshape.111
  29.8 1.3 %fusion.12 = bf16[256,384]{1,0:T(8,128)(2,1)S(1)} fusion(f32[256,384]{1,0:T(8,128)} %get-tuple-element.38, f32[256,384]{1,0:T(8,128)S(1)} %reshape.111, bf16[1,256,384]{2,1,0:T(8,128)(2,1)S(1)} %copy-done.4), kind=kLoop, calls=%fused_computation.33 | loop fusion | flops 2162688 | bytes 1179648 | tf_op jit(solution)/shard_map/convert_element_type | solution.py:462
  31.1 0.3 fusion.25
  31.4 1.0 %convolution_convert_fusion.6 = bf16[384,384]{1,0:T(8,128)(2,1)} fusion(bf16[256,384]{1,0:T(8,128)(2,1)S(1)} %fusion.12, bf16[260,384]{1,0:T(8,128)(2,1)S(1)} %fusion.5), kind=kOutput, calls=%fused_computation.9 | convolution fusion | flops 75644928 | bytes 688128 | tf_op jit(solution)/shard_map/dot_general | solution.py:47
  32.4 1.0 %convolution_convert_fusion.5 = bf16[384,384]{1,0:T(8,128)(2,1)} fusion(bf16[256,384]{1,0:T(8,128)(2,1)S(1)} %fusion.12, bf16[260,384]{1,0:T(8,128)(2,1)S(1)} %fusion.5), kind=kOutput, calls=%fused_computation.8 | convolution fusion | flops 75644928 | bytes 688128 | tf_op jit(solution)/shard_map/dot_general | solution.py:47
  33.4 1.0 %convolution_convert_fusion.4 = bf16[384,384]{1,0:T(8,128)(2,1)} fusion(bf16[256,384]{1,0:T(8,128)(2,1)S(1)} %fusion.12, bf16[260,384]{1,0:T(8,128)(2,1)S(1)} %fusion.5), kind=kOutput, calls=%fused_computation.7 | convolution fusion | flops 75644928 | bytes 688128 | tf_op jit(solution)/shard_map/dot_general | solution.py:47
  34.4 1.0 %convolution_convert_fusion.3 = bf16[384,384]{1,0:T(8,128)(2,1)} fusion(bf16[256,384]{1,0:T(8,128)(2,1)S(1)} %fusion.12, bf16[260,384]{1,0:T(8,128)(2,1)S(1)} %fusion.5), kind=kOutput, calls=%fused_computation.6 | convolution fusion | flops 75644928 | bytes 688128 | tf_op jit(solution)/shard_map/dot_general | solution.py:47
  35.4 1.0 %convolution_convert_fusion.2 = bf16[384,384]{1,0:T(8,128)(2,1)} fusion(bf16[256,384]{1,0:T(8,128)(2,1)S(1)} %fusion.12, bf16[260,384]{1,0:T(8,128)(2,1)S(1)} %fusion.5), kind=kOutput, calls=%fused_computation.5 | convolution fusion | flops 75644928 | bytes 688128 | tf_op jit(solution)/shard_map/dot_general | solution.py:47
  36.5 1.0 fusion.57
  37.4 0.8 broadcast_in_dim.42
  38.3 2.0 %reshape.110 = f32[256,384]{1,0:T(8,128)} reshape(f32[128,2,384]{2,1,0:T(2,128)} %broadcast_in_dim.42) | data formatting | bytes 786432 | tf_op jit(solution)/shard_map/reshape | solution.py:457
  40.3 1.8 %fusion.54 = bf16[1,256,384]{2,1,0:T(8,128)(2,1)} fusion(f32[256,384]{1,0:T(8,128)} %reshape.110, bf16[256,384]{1,0:T(8,128)(2,1)S(1)} %copy-done.6), kind=kLoop, calls=%fused_computation.86 | loop fusion | flops 294912 | bytes 786432 | tf_op jit(solution)/shard_map/broadcast_in_dim | solution.py:476
  42.1 1.3 %collective-permute-start.4 = (bf16[2,384]{1,0:T(2,128)(2,1)S(1)}, bf16[2,384]{1,0:T(2,128)(2,1)S(1)}, u32[]{:S(2)}, u32[]{:S(2)}) collective-permute-start(bf16[2,384]{1,0:T(2,128)(2,1)S(1)} %get-tuple-element.22), channel_id=1, source_target_pairs={{0,2},{1,3},{4,6},{5,7},{8,10},{9,11},{12,14},{13,15},{16,18},{17,... | collective-permute-start | bytes 4616 | tf_op jit(solution)/shard_map/ppermute | solution.py:28
  43.4 1.3 %collective-permute-start.3 = (bf16[2,384]{1,0:T(2,128)(2,1)S(1)}, bf16[2,384]{1,0:T(2,128)(2,1)S(1)}, u32[]{:S(2)}, u32[]{:S(2)}) collective-permute-start(bf16[2,384]{1,0:T(2,128)(2,1)S(1)} %get-tuple-element.21), channel_id=1, source_target_pairs={{2,0},{3,1},{6,4},{7,5},{10,8},{11,9},{14,12},{15,13},{18,16},{19,... | collective-permute-start | bytes 4616 | tf_op jit(solution)/shard_map/ppermute | solution.py:30
  44.7 1.0 constant_dynamic-update-slice_fusion.4
  46.0 0.3 fusion.20
  46.3 0.2 collective-permute-done.3
  46.5 0.3 fusion.28
  46.8 0.3 fusion.3
  47.1 0.3 fusion.4
  47.5 0.3 convolution_convert_fusion.7
  47.7 0.1 reshape.113
  47.8 1.5 %fusion.1 = bf16[2,980,384]{2,1,0:T(8,128)(2,1)S(1)} fusion(bf16[2,20,192]{2,1,0:T(8,128)(2,1)S(1)} %bitcast.94, bf16[2,960,384]{2,1,0:T(8,128)(2,1)} %bitcast.85), kind=kLoop, calls=%fused_computation.2 | loop fusion | flops 4515840 | bytes 2995200 | tf_op jit(solution)/shard_map/concatenate | solution.py:319
  49.4 0.2 pad.9.conv_in
  49.5 47.9 %shard_map.102 = (f32[1024,384]{1,0:T(8,128)S(1)}, f32[384,384]{1,0:T(8,128)S(1)}) custom-call(bf16[2,1024,384]{2,1,0:T(8,128)(2,1)S(1)} %pad.9.conv_in, bf16[2,384,384]{2,1,0:T(8,128)(2,1)S(1)} %pad_maximum_fusion.feed_in), custom_call_target="tpu_custom_call" | custom-call | tf_op jit(solution)/shard_map/pallas_call | solution.py:264
  97.4 1.2 %slice.138 = f32[960,384]{1,0:T(8,128)} slice(f32[1024,384]{1,0:T(8,128)S(1)} %get-tuple-element.17), slice={[0:960], [0:384]} | slice | bytes 2949120 | tf_op jit(solution)/shard_map/slice | solution.py:326
  98.6 0.6 reshape.116
  99.3 0.8 slice_bitcast_fusion
  (47 shorter events, 0.6 us)
Async XLA Ops:
  0.6 12.0 %copy-start.15 = (bf16[5,4,384]{2,1,0:T(4,128)(2,1)S(1)}, bf16[5,4,384]{2,1,0:T(4,128)(2,1)}, u32[]{:S(2)}) copy-start(bf16[5,4,384]{2,1,0:T(4,128)(2,1)} %param.7) | copy-start | bytes 46084
  2.9 1.1 %copy-start = (bf16[5,192,384]{2,1,0:T(8,128)(2,1)S(1)}, bf16[5,192,384]{2,1,0:T(8,128)(2,1)}, u32[]{:S(2)}) copy-start(bf16[5,192,384]{2,1,0:T(8,128)(2,1)} %conv_w.1) | copy-start | bytes 2211844
  4.0 0.9 copy-start.1
  4.9 0.9 copy-start.2
  12.8 1.1 %copy-start.13 = (pred[260,20]{0,1:T(8,128)(4,1)}, pred[260,20]{0,1:T(8,128)(4,1)S(1)}, u32[]{:S(2)}) copy-start(pred[260,20]{0,1:T(8,128)(4,1)S(1)} %concatenate.38) | copy-start | bytes 15604
  15.4 0.7 copy-start.5
  17.0 4.7 %collective-permute-start = (bf16[128,384]{1,0:T(8,128)(2,1)S(1)}, bf16[128,384]{1,0:T(8,128)(2,1)S(1)}, u32[]{:S(2)}, u32[]{:S(2)}) collective-permute-start(bf16[128,384]{1,0:T(8,128)(2,1)S(1)} %fusion.49), channel_id=1, source_target_pairs={{0,1},{1,0},{2,3},{3,2},{4,5},{5,4},{6,7},{7,6},{8,9},{9,8},{10,11... | collective-permute-start | bytes 294920 | tf_op jit(solution)/shard_map/ppermute | solution.py:17
  22.5 1.6 %copy-start.11 = (f32[256,384]{1,0:T(8,128)}, f32[256,384]{1,0:T(8,128)S(1)}, u32[]{:S(2)}) copy-start(f32[256,384]{1,0:T(8,128)S(1)} %fusion.81) | copy-start | bytes 1179652
  22.9 13.6 %collective-permute-start.1 = (bf16[128,384]{1,0:T(8,128)(2,1)S(1)}, bf16[128,384]{1,0:T(8,128)(2,1)}, u32[]{:S(2)}, u32[]{:S(2)}) collective-permute-start(bf16[128,384]{1,0:T(8,128)(2,1)S(1)} %slice.247), channel_id=1, source_target_pairs={{0,1},{1,0},{2,3},{3,2},{4,5},{5,4},{6,7},{7,6},{8,9},{9,8},{10,11... | collective-permute-start | bytes 294920 | tf_op jit(solution)/shard_map/ppermute | solution.py:17
  24.4 4.7 %collective-permute-start.2 = (bf16[128,384]{1,0:T(8,128)(2,1)S(1)}, bf16[128,384]{1,0:T(8,128)(2,1)S(1)}, u32[]{:S(2)}, u32[]{:S(2)}) collective-permute-start(bf16[128,384]{1,0:T(8,128)(2,1)S(1)} %slice.246), channel_id=1, source_target_pairs={{0,1},{1,0},{2,3},{3,2},{4,5},{5,4},{6,7},{7,6},{8,9},{9,8},{10,11... | collective-permute-start | bytes 294920 | tf_op jit(solution)/shard_map/ppermute | solution.py:17
  25.7 4.0 %copy-start.4 = (bf16[1,256,384]{2,1,0:T(8,128)(2,1)S(1)}, bf16[1,256,384]{2,1,0:T(8,128)(2,1)}, u32[]{:S(2)}) copy-start(bf16[1,256,384]{2,1,0:T(8,128)(2,1)} %param.11) | copy-start | bytes 589828
  33.4 3.1 %copy-start.12 = (f32[256,384]{1,0:T(8,128)S(1)}, f32[256,384]{1,0:T(8,128)}, u32[]{:S(2)}) copy-start(f32[256,384]{1,0:T(8,128)} %copy-done.11) | copy-start | bytes 1179652
  36.4 3.9 %copy-start.6 = (bf16[256,384]{1,0:T(8,128)(2,1)S(1)}, bf16[256,384]{1,0:T(8,128)(2,1)}, u32[]{:S(2)}) copy-start(bf16[256,384]{1,0:T(8,128)(2,1)} %copy-done.5) | copy-start | bytes 589828
  40.3 5.4 %copy-start.10 = (bf16[384,384]{1,0:T(8,128)(2,1)S(1)}, bf16[384,384]{1,0:T(8,128)(2,1)}, u32[]{:S(2)}) copy-start(bf16[384,384]{1,0:T(8,128)(2,1)} %convolution_convert_fusion.5) | copy-start | bytes 884740
  40.3 5.5 %copy-start.9 = (bf16[384,384]{1,0:T(8,128)(2,1)S(1)}, bf16[384,384]{1,0:T(8,128)(2,1)}, u32[]{:S(2)}) copy-start(bf16[384,384]{1,0:T(8,128)(2,1)} %convolution_convert_fusion.4) | copy-start | bytes 884740
  40.3 5.5 %copy-start.8 = (bf16[384,384]{1,0:T(8,128)(2,1)S(1)}, bf16[384,384]{1,0:T(8,128)(2,1)}, u32[]{:S(2)}) copy-start(bf16[384,384]{1,0:T(8,128)(2,1)} %convolution_convert_fusion.3) | copy-start | bytes 884740
  40.3 5.6 %copy-start.7 = (bf16[384,384]{1,0:T(8,128)(2,1)S(1)}, bf16[384,384]{1,0:T(8,128)(2,1)}, u32[]{:S(2)}) copy-start(bf16[384,384]{1,0:T(8,128)(2,1)} %convolution_convert_fusion.2) | copy-start | bytes 884740
  42.1 3.9 %collective-permute-start.4 = (bf16[2,384]{1,0:T(2,128)(2,1)S(1)}, bf16[2,384]{1,0:T(2,128)(2,1)S(1)}, u32[]{:S(2)}, u32[]{:S(2)}) collective-permute-start(bf16[2,384]{1,0:T(2,128)(2,1)S(1)} %get-tuple-element.22), channel_id=1, source_target_pairs={{0,2},{1,3},{4,6},{5,7},{8,10},{9,11},{12,14},{13,15},{16,18},{17,... | collective-permute-start | bytes 4616 | tf_op jit(solution)/shard_map/ppermute | solution.py:28
  43.4 3.0 %collective-permute-start.3 = (bf16[2,384]{1,0:T(2,128)(2,1)S(1)}, bf16[2,384]{1,0:T(2,128)(2,1)S(1)}, u32[]{:S(2)}, u32[]{:S(2)}) collective-permute-start(bf16[2,384]{1,0:T(2,128)(2,1)S(1)} %get-tuple-element.21), channel_id=1, source_target_pairs={{2,0},{3,1},{6,4},{7,5},{10,8},{11,9},{14,12},{15,13},{18,16},{19,... | collective-permute-start | bytes 4616 | tf_op jit(solution)/shard_map/ppermute | solution.py:30
  46.0 1.1 %copy-start.3 = (bf16[5,2,192,384]{3,2,0,1:T(8,128)(2,1)}, bf16[5,2,192,384]{3,2,0,1:T(8,128)(2,1)S(1)}, u32[]{:S(2)}) copy-start(bf16[5,2,192,384]{3,2,0,1:T(8,128)(2,1)S(1)} %constant_dynamic-update-slice_fusion) | copy-start | bytes 4423684
  46.8 0.7 copy-start.14

commit v3 on v2

--- a/solution.py
+++ b/solution.py
@@ -74,21 +74,13 @@
     )
 
 
-def reduce_kernel(
-    seqs, high, conv_in, feed_in, conv_out, feed_out,
-    conv_r0, feed_r0, conv_a1, feed_a1, conv_r1, feed_r1, conv_a2, feed_a2,
-    conv_r2, feed_r2, conv_all, feed_all,
-    s0, r0, s1, r1, s2, r2, s3, r3, s4, r4,
-):
+def reduce_kernel(seqs, high, conv_in, feed_in, conv_out, feed_out, send, recv, *buffers):
     me_seq = lax.axis_index("seq")
     me_sect = lax.axis_index("sect")
     me_dp = lax.axis_index("dp")
     low = lax.rem(me_dp, 2)
     up = me_dp // 2
     quad = me_sect * 2 + low
-    conv_block, feed_block = conv_a2.shape[0], feed_a2.shape[0]
-    conv_piece, feed_piece = conv_r2.shape[1], feed_r2.shape[1]
-
     seq_ids = [lax.rem(me_seq + k, seqs) for k in range(1, seqs)]
     quad_ids = [(k // 2, k % 2) for k in range(1, 4)]
     quad_ids = [
@@ -126,141 +118,132 @@
 
         lax.fori_loop(0, count, body, 0)
 
-    copies = []
-    for k in range(seqs - 1):
-        copies.append(
-            remote(conv_in.at[seq_ids[k]], conv_r0.at[k], s0.at[0, k], r0.at[0, k], seq_place[k])
-        )
-        copies.append(
-            remote(feed_in.at[seq_ids[k]], feed_r0.at[k], s0.at[1, k], r0.at[1, k], seq_place[k])
-        )
-    for copy in copies:
-        copy.start()
-    finish(copies)
-    total(4 * high, conv_piece, conv_a1, lambda at: conv_in[me_seq, at], conv_r0)
-    total(2 * high, feed_piece, feed_a1, lambda at: feed_in[me_seq, at], feed_r0)
-
-    copies = []
-    for k in (2, 1, 0):
-        a, b = quad_ids[k]
-        copies.append(
-            remote(
-                conv_a1.at[rows(a * 2 + b, conv_block)],
-                conv_r1.at[k],
-                s1.at[k],
-                r1.at[k],
-                quad_place[k],
-            )
-        )
-    copies.append(
-        remote(
-            feed_a1.at[rows(quad_ids[0][1], feed_block)],
-            feed_r1.at[0],
-            s1.at[3],
-            r1.at[3],
-            quad_place[0],
-        )
-    )
-    for copy in copies:
-        copy.start()
-    finish(copies)
-    conv_at, feed_at = quad * conv_block, low * feed_block
-
-    def own_conv(at):
-        return conv_a1[pl.ds(pl.multiple_of(conv_at + at.start, conv_piece), conv_piece)]
-
-    def own_feed(at):
-        return feed_a1[pl.ds(pl.multiple_of(feed_at + at.start, feed_piece), feed_piece)]
-
-    total(high, conv_piece, conv_a2, own_conv, conv_r1)
-    total(high, feed_piece, feed_a2, own_feed, feed_r1)
-
-    copies = []
-    for k in range(high - 1):
-        copies.append(
-            remote(
-                conv_a2.at[rows(high_ids[k], conv_piece)],
-                conv_r2.at[k],
-                s2.at[0, k],
-                r2.at[0, k],
-                high_place[k],
-            )
-        )
-        copies.append(
-            remote(
-                feed_a2.at[rows(high_ids[k], feed_piece)],
-                feed_r2.at[k],
-                s2.at[1, k],
-                r2.at[1, k],
-                high_place[k],
-            )
-        )
-    for copy in copies:
-        copy.start()
-    finish(copies)
-    conv_mine = rows(quad * high + up, conv_piece)
-    feed_mine = rows(low * high + up, feed_piece)
-    value = conv_a2[rows(up, conv_piece)].astype(jnp.float32)
-    for k in range(high - 1):
-        value = value + conv_r2[k].astype(jnp.float32)
-    conv_all[conv_mine] = value.astype(jnp.bfloat16)
-    value = feed_a2[rows(up, feed_piece)].astype(jnp.float32)
-    for k in range(high - 1):
-        value = value + feed_r2[k].astype(jnp.float32)
-    feed_all[feed_mine] = value.astype(jnp.bfloat16)
-
-    copies = []
-    for k in range(high - 1):
-        copies.append(
-            remote(
-                conv_all.at[conv_mine], conv_all.at[conv_mine],
-                s3.at[0, k], r3.at[0, k], high_place[k],
-            )
-        )
-        copies.append(
-            remote(
-                feed_all.at[feed_mine], feed_all.at[feed_mine],
-                s3.at[1, k], r3.at[1, k], high_place[k],
-            )
-        )
-    for copy in copies:
-        copy.start()
-    finish(copies)
-
-    copies = []
-    for k in (2, 1, 0):
-        mine = conv_all.at[rows(quad, conv_block)]
-        copies.append(remote(mine, mine, s4.at[k], r4.at[k], quad_place[k]))
-    mine = feed_all.at[rows(low, feed_block)]
-    copies.append(remote(mine, mine, s4.at[3], r4.at[3], quad_place[0]))
-    for copy in copies:
-        copy.start()
-    finish(copies)
-
-    def widen(count, size, dest, source):
+    quads = (quad, [(a * 2 + b, p) for (a, b), p in zip(quad_ids, quad_place)])
+    highs = (up, list(zip(high_ids, high_place)))
+    lows = (low, [(quad_ids[0][1], quad_place[0])])
+    half = conv_in.shape[1] // 2
+    plans = [
+        (conv_in, conv_out, 0, quads, highs),
+        (conv_in, conv_out, half, highs, quads),
+        (feed_in, feed_out, 0, lows, highs),
+    ]
+    streams = [plan + tuple(buffers[6 * n : 6 * n + 6]) for n, plan in enumerate(plans)]
+
+    def exchange(phase, pairs):
+        copies = []
+        for n, stream in enumerate(streams):
+            for k, (src, dst, place) in enumerate(pairs(stream)):
+                at = n * 5 + phase, k
+                copies.append(remote(src, dst, send.at[at], recv.at[at], place))
+        for copy in copies:
+            copy.start()
+        finish(copies)
+
+    def scatter_seq(stream):
+        source, out, base, first, second, r0, a1, r1, a2, r2, full = stream
+        return [
+            (source.at[peer, pl.ds(base, a1.shape[0])], r0.at[k], place)
+            for k, (peer, place) in enumerate(zip(seq_ids, seq_place))
+        ]
+
+    def scatter_first(stream):
+        source, out, base, first, second, r0, a1, r1, a2, r2, full = stream
+        return [
+            (a1.at[rows(peer, a2.shape[0])], r1.at[k], place)
+            for k, (peer, place) in enumerate(first[1])
+        ]
+
+    def scatter_second(stream):
+        source, out, base, first, second, r0, a1, r1, a2, r2, full = stream
+        return [
+            (a2.at[rows(peer, r2.shape[1])], r2.at[k], place)
+            for k, (peer, place) in enumerate(second[1])
+        ]
+
+    def mine_of(stream):
+        source, out, base, first, second, r0, a1, r1, a2, r2, full = stream
+        piece = r2.shape[1]
+        return rows(first[0] * (a2.shape[0] // piece) + second[0], piece)
+
+    def gather_second(stream):
+        part = stream[-1].at[mine_of(stream)]
+        return [(part, part, place) for peer, place in stream[4][1]]
+
+    def gather_first(stream):
+        part = stream[-1].at[rows(stream[3][0], stream[8].shape[0])]
+        return [(part, part, place) for peer, place in stream[3][1]]
+
+    def add(piece, count, dest, own, slots):
         def body(i, carry):
-            at = rows(i, size)
-            dest[at] = source[at].astype(jnp.float32)
+            at = rows(i, piece)
+            value = own(i * piece, piece).astype(jnp.float32)
+            for slot in range(slots.shape[0]):
+                value = value + slots[slot, at].astype(jnp.float32)
+            dest[at] = value.astype(dest.dtype)
             return carry
 
         lax.fori_loop(0, count, body, 0)
 
-    widen(4 * high, conv_piece, conv_out, conv_all)
-    widen(2 * high, feed_piece, feed_out, feed_all)
+    def at_rows(start, size):
+        return pl.ds(pl.multiple_of(start, 16), size)
+
+    exchange(0, scatter_seq)
+    for source, out, base, first, second, r0, a1, r1, a2, r2, full in streams:
+        piece = r2.shape[1]
+        add(
+            piece, a1.shape[0] // piece, a1,
+            lambda at, size, source=source, base=base: source[me_seq, at_rows(base + at, size)],
+            r0,
+        )
+    exchange(1, scatter_first)
+    for source, out, base, first, second, r0, a1, r1, a2, r2, full in streams:
+        piece, start = r2.shape[1], first[0] * a2.shape[0]
+        add(
+            piece, a2.shape[0] // piece, a2,
+            lambda at, size, a1=a1, start=start: a1[at_rows(start + at, size)],
+            r1,
+        )
+    exchange(2, scatter_second)
+    for stream in streams:
+        a2, r2, full = stream[-3:]
+        value = a2[rows(stream[4][0], r2.shape[1])].astype(jnp.float32)
+        for k in range(r2.shape[0]):
+            value = value + r2[k].astype(jnp.float32)
+        full[mine_of(stream)] = value.astype(jnp.bfloat16)
+    exchange(3, gather_second)
+    exchange(4, gather_first)
+    for source, out, base, first, second, r0, a1, r1, a2, r2, full in streams:
+        piece = r2.shape[1]
+
+        def widen(i, carry, out=out, base=base, full=full, piece=piece):
+            out[at_rows(base + i * piece, piece)] = full[rows(i, piece)].astype(jnp.float32)
+            return carry
+
+        lax.fori_loop(0, full.shape[0] // piece, widen, 0)
 
 
 def summed(conv_pack, feed_pack):
     seqs = lax.axis_size("seq")
     high = lax.axis_size("dp") // 2
     conv_rows, feed_rows, cols = conv_pack.shape[1], feed_pack.shape[1], conv_pack.shape[2]
-    conv_block, feed_block = conv_rows // 4, feed_rows // 2
-    conv_piece, feed_piece = conv_block // high, feed_block // high
     low = jnp.bfloat16
 
     def buffer(*shape):
         return pltpu.VMEM(shape + (cols,), low)
 
+    def stream(count, first, second):
+        block = count // first
+        return [
+            buffer(seqs - 1, count),
+            buffer(count),
+            buffer(first - 1, block),
+            buffer(block),
+            buffer(second - 1, block // second),
+            buffer(count),
+        ]
+
     dma = pltpu.SemaphoreType.DMA
+    peers = max(seqs - 1, 3, high - 1)
     return pl.pallas_call(
         functools.partial(reduce_kernel, seqs, high),
         out_shape=(
@@ -270,28 +253,11 @@
         in_specs=[pl.BlockSpec(memory_space=pltpu.VMEM)] * 2,
         out_specs=[pl.BlockSpec(memory_space=pltpu.VMEM)] * 2,
         scratch_shapes=[
-            buffer(seqs - 1, conv_rows),
-            buffer(seqs - 1, feed_rows),
-            buffer(conv_rows),
-            buffer(feed_rows),
-            buffer(3, conv_block),
-            buffer(1, feed_block),
-            buffer(conv_block),
-            buffer(feed_block),
-            buffer(high - 1, conv_piece),
-            buffer(high - 1, feed_piece),
-            buffer(conv_rows),
-            buffer(feed_rows),
-            dma((2, seqs - 1)),
-            dma((2, seqs - 1)),
-            dma((4,)),
-            dma((4,)),
-            dma((2, high - 1)),
-            dma((2, high - 1)),
-            dma((2, high - 1)),
-            dma((2, high - 1)),
-            dma((4,)),
-            dma((4,)),
+            dma((15, peers)),
+            dma((15, peers)),
+            *stream(conv_rows // 2, 4, high),
+            *stream(conv_rows // 2, high, 4),
+            *stream(feed_rows, 2, high),
         ],
         compiler_params=pltpu.CompilerParams(
             collective_id=0, has_side_effects=True, vmem_limit_bytes=40 * 2**20
@@ -316,7 +282,7 @@
     kinds = taps * BASES
     embed_pack = embed_term.astype(low).reshape(kinds, seqs, part).transpose(1, 0, 2)
     embed_pack = jnp.pad(embed_pack, ((0, 0), (0, 0), (0, chans - part)))
-    conv_pack = padded_rows(jnp.concatenate([conv_pack, embed_pack], axis=1), 2 * dps)
+    conv_pack = padded_rows(jnp.concatenate([conv_pack, embed_pack], axis=1), 4 * dps)
     feed_pack = jnp.concatenate(
         [in_term.astype(low).reshape(seqs, part, hidden), out_term.astype(low).reshape(seqs, part, hidden)],
         axis=1,

time: 102 us -> 91.2 us (0.89); the launches traced: 100 us -> 90.7 us
  Pallas kernels: 54.4 us -> 45 us
    pallas_call x1, Pallas kernels: 47.9 us -> 38.4 us  [summed(): pl.pallas_call(functools.partial(reduce_kernel, seqs, high), out_shape=(j...]
  transfers between devices with their start and end apart: 5 -> 5, of which waited for: 3 -> 3; matrix products, arithmetic and copies ran while one was open for 10% -> 11% of each run, Pallas kernels for 0% -> 0%
where the time goes in v3:
time: 91.2 us; the launch traced here: 90.7 us
  Pallas kernels  45 us (49%)
  local copies, waits for them, and re-layouts  12.4 us (14%)
  matrix products  11.4 us (12%)
  other arithmetic  8.12 us (9%)
  waiting for transfers between devices  6.72 us (7%)
  starting transfers between devices  5.94 us (7%)
  between operations  1.14 us (1%)
    pallas_call x1, Pallas kernels, summed(): pl.pallas_call(functools.partial(reduce_kernel, seqs, high), out_shape=(j...  38.4 us
    ppermute x3, waiting for transfers between devices, swapped(): return lax.ppermute(value, axis, pairs)  6.56 us
    pallas_call x1, Pallas kernels, gathered(): pl.pallas_call(functools.partial(gather_kernel, seqs), out_shape=(jax.Sha...  6.55 us
    dot_general x7, matrix products, contract_rows(): lax.dot_general(left, right, (((0,), (0,)), ((), ())), preferred_element_...  5.75 us
    unnamed x36, local copies, waits for them, and re-layouts  4.84 us
    ppermute x3, starting transfers between devices, swapped(): return lax.ppermute(value, axis, pairs)  3.37 us
    dot_general x5, matrix products, local(): jnp.dot(h_padded[k:k + rows], conv_full[k], preferred_element_type=jnp.fl...  2.23 us
    dot_general x7, matrix products, contract_cols(): lax.dot_general(left, right, (((1,), (1,)), ((), ())), preferred_element_...  2.1 us
  transfers between devices with their start and end apart: 5, of which 3 were waited for; matrix products, arithmetic and copies ran while one was open for 11% of the time, Pallas kernels for 0%

profile of v3, /device:TPU:0, one launch (start us, length us, event | category | flops | bytes accessed | tf_op | source)
XLA Modules:
  0.0 90.7 jit_solution(2283593694593579680)
XLA Ops:
  0.7 0.7 broadcast_add_fusion.ids
  1.3 1.0 %squeeze.28 = bf16[128,2,384]{2,1,0:T(2,128)(2,1)S(1)} reshape(bf16[1,256,384]{2,1,0:T(8,128)(2,1)} %param.11) | data formatting | bytes 393216 | tf_op jit(solution)/shard_map/squeeze | solution.py:372
  2.4 0.5 reduce_sum.39.dmixed
  2.9 1.1 %copy-done = bf16[5,192,384]{2,1,0:T(8,128)(2,1)S(1)} copy-done((bf16[5,192,384]{2,1,0:T(8,128)(2,1)S(1)}, bf16[5,192,384]{2,1,0:T(8,128)(2,1)}, u32[]{:S(2)}) %copy-start) | copy-done | bytes 737304
  4.0 0.9 %copy-done.1 = bf16[192,384]{1,0:T(8,128)(2,1)S(1)} copy-done((bf16[192,384]{1,0:T(8,128)(2,1)S(1)}, bf16[192,384]{1,0:T(8,128)(2,1)}, u32[]{:S(2)}) %copy-start.1) | copy-done | bytes 147480
  4.9 0.9 %copy-done.2 = bf16[384,192]{0,1:T(8,128)(2,1)S(1)} copy-done((bf16[384,192]{0,1:T(8,128)(2,1)S(1)}, bf16[384,192]{0,1:T(8,128)(2,1)}, u32[]{:S(2)}) %copy-start.2) | copy-done | bytes 147480
  5.8 6.6 %shard_map.101 = (bf16[5,384,384]{2,1,0:T(8,128)(2,1)S(1)}, bf16[384,384]{1,0:T(8,128)(2,1)S(1)}, bf16[384,384]{1,0:T(8,128)(2,1)S(1)}, s32[2,1,256]{2,1,0:T(1,128)S(1)}, bf16[256,384]{1,0:T(8,128)(2,1)S(1)}) custom-call(bf16[5,192,384]{2,1,0:T(8,128)(2,1)S(1)} %copy-done, bf16[192,384]{1,0:T(8,128)(2,1)S(1)} %copy-done.1, bf16[192,384]{1,0:T(8,128)(2,1)S(1)} %bitcast.82, ...), custom_call_target="tpu_custom_call" | custom-call | tf_op jit(solution)/shard_map/pallas_call | solution.py:341
  12.4 0.1 pad_add_fusion.1
  12.5 0.1 pad_add_fusion.2
  12.6 0.1 broadcast_compare_fusion
  12.7 0.1 concatenate.38
  12.8 0.3 fusion.5
  13.1 0.3 fusion.32
  13.4 0.3 convolution_add_fusion.5
  13.6 0.3 convolution_add_fusion.4
  13.9 0.3 convolution_add_fusion.3
  14.2 1.1 %add_convert_fusion.1 = (bf16[256,384]{1,0:T(8,128)(2,1)S(1)}, f32[256,384]{1,0:T(8,128)}) fusion(bf16[260,384]{1,0:T(8,128)(2,1)S(1)} %fusion.5, f32[256,384]{1,0:T(8,128)S(1)} %convolution_add_fusion.3, bf16[5,384,384]{2,1,0:T(8,128)(2,1)S(1)} %get-tuple-element.13), kind=kOutput, calls=%fused_computation.44 | convolution fusion | flops 76677120 | bytes 1671168 | tf_op jit(solution)/shard_map/dot_general | solution.py:397
  15.4 0.7 copy-done.5
  16.0 0.2 reshape.109
  16.2 0.5 reduce_sum.40
  16.7 0.1 fusion.48
  16.9 0.1 fusion.49
  17.0 1.2 %collective-permute-start = (bf16[128,384]{1,0:T(8,128)(2,1)S(1)}, bf16[128,384]{1,0:T(8,128)(2,1)S(1)}, u32[]{:S(2)}, u32[]{:S(2)}) collective-permute-start(bf16[128,384]{1,0:T(8,128)(2,1)S(1)} %fusion.49), channel_id=1, source_target_pairs={{0,1},{1,0},{2,3},{3,2},{4,5},{5,4},{6,7},{7,6},{8,9},{9,8},{10,11... | collective-permute-start | bytes 294920 | tf_op jit(solution)/shard_map/ppermute | solution.py:17
  18.2 0.3 fusion.84
  18.4 3.2 %collective-permute-done = bf16[128,384]{1,0:T(8,128)(2,1)S(1)} collective-permute-done((bf16[128,384]{1,0:T(8,128)(2,1)S(1)}, bf16[128,384]{1,0:T(8,128)(2,1)S(1)}, u32[]{:S(2)}, u32[]{:S(2)}) %collective-permute-start) | collective-permute-done | bytes 98336 | tf_op jit(solution)/shard_map/ppermute | solution.py:17
  21.6 0.5 fusion.19
  22.1 0.3 fusion.81
  22.5 0.4 convolution_convert_fusion
  22.9 1.2 %collective-permute-start.1 = (bf16[128,384]{1,0:T(8,128)(2,1)S(1)}, bf16[128,384]{1,0:T(8,128)(2,1)}, u32[]{:S(2)}, u32[]{:S(2)}) collective-permute-start(bf16[128,384]{1,0:T(8,128)(2,1)S(1)} %slice.247), channel_id=1, source_target_pairs={{0,1},{1,0},{2,3},{3,2},{4,5},{5,4},{6,7},{7,6},{8,9},{9,8},{10,11... | collective-permute-start | bytes 294920 | tf_op jit(solution)/shard_map/ppermute | solution.py:17
  24.1 0.3 fusion.85
  24.4 1.0 %collective-permute-start.2 = (bf16[128,384]{1,0:T(8,128)(2,1)S(1)}, bf16[128,384]{1,0:T(8,128)(2,1)S(1)}, u32[]{:S(2)}, u32[]{:S(2)}) collective-permute-start(bf16[128,384]{1,0:T(8,128)(2,1)S(1)} %slice.246), channel_id=1, source_target_pairs={{0,1},{1,0},{2,3},{3,2},{4,5},{5,4},{6,7},{7,6},{8,9},{9,8},{10,11... | collective-permute-start | bytes 294920 | tf_op jit(solution)/shard_map/ppermute | solution.py:17
  25.3 0.3 convolution_convert_fusion.1
  25.7 3.4 %collective-permute-done.2 = bf16[128,384]{1,0:T(8,128)(2,1)S(1)} collective-permute-done((bf16[128,384]{1,0:T(8,128)(2,1)S(1)}, bf16[128,384]{1,0:T(8,128)(2,1)S(1)}, u32[]{:S(2)}, u32[]{:S(2)}) %collective-permute-start.2) | collective-permute-done | bytes 98336 | tf_op jit(solution)/shard_map/ppermute | solution.py:17
  29.1 0.1 fusion.53
  29.2 0.1 fusion.52
  29.3 0.1 broadcast_in_dim.44
  29.5 0.3 reshape.111
  29.8 1.3 %fusion.12 = bf16[256,384]{1,0:T(8,128)(2,1)S(1)} fusion(f32[256,384]{1,0:T(8,128)} %get-tuple-element.38, f32[256,384]{1,0:T(8,128)S(1)} %reshape.111, bf16[1,256,384]{2,1,0:T(8,128)(2,1)S(1)} %copy-done.4), kind=kLoop, calls=%fused_computation.33 | loop fusion | flops 2162688 | bytes 1179648 | tf_op jit(solution)/shard_map/convert_element_type | solution.py:428
  31.1 0.3 fusion.25
  31.4 1.0 %convolution_convert_fusion.6 = bf16[384,384]{1,0:T(8,128)(2,1)} fusion(bf16[256,384]{1,0:T(8,128)(2,1)S(1)} %fusion.12, bf16[260,384]{1,0:T(8,128)(2,1)S(1)} %fusion.5), kind=kOutput, calls=%fused_computation.9 | convolution fusion | flops 75644928 | bytes 688128 | tf_op jit(solution)/shard_map/dot_general | solution.py:47
  32.4 1.0 %convolution_convert_fusion.5 = bf16[384,384]{1,0:T(8,128)(2,1)} fusion(bf16[256,384]{1,0:T(8,128)(2,1)S(1)} %fusion.12, bf16[260,384]{1,0:T(8,128)(2,1)S(1)} %fusion.5), kind=kOutput, calls=%fused_computation.8 | convolution fusion | flops 75644928 | bytes 688128 | tf_op jit(solution)/shard_map/dot_general | solution.py:47
  33.4 1.0 %convolution_convert_fusion.4 = bf16[384,384]{1,0:T(8,128)(2,1)} fusion(bf16[256,384]{1,0:T(8,128)(2,1)S(1)} %fusion.12, bf16[260,384]{1,0:T(8,128)(2,1)S(1)} %fusion.5), kind=kOutput, calls=%fused_computation.7 | convolution fusion | flops 75644928 | bytes 688128 | tf_op jit(solution)/shard_map/dot_general | solution.py:47
  34.4 1.0 %convolution_convert_fusion.3 = bf16[384,384]{1,0:T(8,128)(2,1)} fusion(bf16[256,384]{1,0:T(8,128)(2,1)S(1)} %fusion.12, bf16[260,384]{1,0:T(8,128)(2,1)S(1)} %fusion.5), kind=kOutput, calls=%fused_computation.6 | convolution fusion | flops 75644928 | bytes 688128 | tf_op jit(solution)/shard_map/dot_general | solution.py:47
  35.4 1.0 %convolution_convert_fusion.2 = bf16[384,384]{1,0:T(8,128)(2,1)} fusion(bf16[256,384]{1,0:T(8,128)(2,1)S(1)} %fusion.12, bf16[260,384]{1,0:T(8,128)(2,1)S(1)} %fusion.5), kind=kOutput, calls=%fused_computation.5 | convolution fusion | flops 75644928 | bytes 688128 | tf_op jit(solution)/shard_map/dot_general | solution.py:47
  36.5 1.0 %fusion.57 = bf16[128,384]{1,0:T(8,128)(2,1)S(1)} fusion(f32[256,384]{1,0:T(8,128)S(1)} %copy-done.12, bf16[128,384]{1,0:T(8,128)(2,1)} %collective-permute-done.1), kind=kLoop, calls=%fused_computation.95 | loop fusion | flops 147456 | bytes 393216 | tf_op jit(solution)/shard_map/convert_element_type | solution.py:415
  37.4 0.8 broadcast_in_dim.42
  38.3 2.0 %reshape.110 = f32[256,384]{1,0:T(8,128)} reshape(f32[128,2,384]{2,1,0:T(2,128)} %broadcast_in_dim.42) | data formatting | bytes 786432 | tf_op jit(solution)/shard_map/reshape | solution.py:423
  40.3 1.8 %fusion.54 = bf16[1,256,384]{2,1,0:T(8,128)(2,1)} fusion(f32[256,384]{1,0:T(8,128)} %reshape.110, bf16[256,384]{1,0:T(8,128)(2,1)S(1)} %copy-done.6), kind=kLoop, calls=%fused_computation.86 | loop fusion | flops 294912 | bytes 786432 | tf_op jit(solution)/shard_map/broadcast_in_dim | solution.py:442
  42.1 1.3 %collective-permute-start.4 = (bf16[2,384]{1,0:T(2,128)(2,1)S(1)}, bf16[2,384]{1,0:T(2,128)(2,1)S(1)}, u32[]{:S(2)}, u32[]{:S(2)}) collective-permute-start(bf16[2,384]{1,0:T(2,128)(2,1)S(1)} %get-tuple-element.22), channel_id=1, source_target_pairs={{0,2},{1,3},{4,6},{5,7},{8,10},{9,11},{12,14},{13,15},{16,18},{17,... | collective-permute-start | bytes 4616 | tf_op jit(solution)/shard_map/ppermute | solution.py:28
  43.4 1.3 %collective-permute-start.3 = (bf16[2,384]{1,0:T(2,128)(2,1)S(1)}, bf16[2,384]{1,0:T(2,128)(2,1)S(1)}, u32[]{:S(2)}, u32[]{:S(2)}) collective-permute-start(bf16[2,384]{1,0:T(2,128)(2,1)S(1)} %get-tuple-element.21), channel_id=1, source_target_pairs={{2,0},{3,1},{6,4},{7,5},{10,8},{11,9},{14,12},{15,13},{18,16},{19,... | collective-permute-start | bytes 4616 | tf_op jit(solution)/shard_map/ppermute | solution.py:30
  44.7 1.0 %constant_dynamic-update-slice_fusion.4 = bf16[5,2,192,384]{3,2,0,1:T(8,128)(2,1)S(1)} fusion(bf16[1,2,192,384]{3,2,0,1:T(8,128)(2,1)} %bitcast.87), kind=kLoop, calls=%fused_computation.115 | loop fusion | bytes 589824
  46.0 0.3 fusion.20
  46.3 0.2 collective-permute-done.3
  46.5 0.3 fusion.28
  46.8 0.3 fusion.3
  47.1 0.3 fusion.4
  47.5 0.3 convolution_convert_fusion.7
  47.7 0.1 reshape.113
  47.8 1.5 %fusion.1 = bf16[2,980,384]{2,1,0:T(8,128)(2,1)S(1)} fusion(bf16[2,20,192]{2,1,0:T(8,128)(2,1)S(1)} %bitcast.94, bf16[2,960,384]{2,1,0:T(8,128)(2,1)} %bitcast.85), kind=kLoop, calls=%fused_computation.2 | loop fusion | flops 4515840 | bytes 2995200 | tf_op jit(solution)/shard_map/concatenate | solution.py:285
  49.4 0.2 pad.9.conv_in
  49.5 38.4 %shard_map.102 = (f32[1024,384]{1,0:T(8,128)S(1)}, f32[384,384]{1,0:T(8,128)S(1)}) custom-call(bf16[2,1024,384]{2,1,0:T(8,128)(2,1)S(1)} %pad.9.conv_in, bf16[2,384,384]{2,1,0:T(8,128)(2,1)S(1)} %pad_maximum_fusion.feed_in), custom_call_target="tpu_custom_call" | custom-call | tf_op jit(solution)/shard_map/pallas_call | solution.py:247
  88.0 1.2 %slice.138 = f32[960,384]{1,0:T(8,128)} slice(f32[1024,384]{1,0:T(8,128)S(1)} %get-tuple-element.17), slice={[0:960], [0:384]} | slice | bytes 2949120 | tf_op jit(solution)/shard_map/slice | solution.py:292
  89.2 0.6 reshape.116
  89.8 0.8 slice_bitcast_fusion
  (47 shorter events, 0.6 us)
Async XLA Ops:
  0.6 12.0 %copy-start.15 = (bf16[5,4,384]{2,1,0:T(4,128)(2,1)S(1)}, bf16[5,4,384]{2,1,0:T(4,128)(2,1)}, u32[]{:S(2)}) copy-start(bf16[5,4,384]{2,1,0:T(4,128)(2,1)} %param.7) | copy-start | bytes 46084
  2.9 1.1 %copy-start = (bf16[5,192,384]{2,1,0:T(8,128)(2,1)S(1)}, bf16[5,192,384]{2,1,0:T(8,128)(2,1)}, u32[]{:S(2)}) copy-start(bf16[5,192,384]{2,1,0:T(8,128)(2,1)} %conv_w.1) | copy-start | bytes 2211844
  4.0 0.9 %copy-start.1 = (bf16[192,384]{1,0:T(8,128)(2,1)S(1)}, bf16[192,384]{1,0:T(8,128)(2,1)}, u32[]{:S(2)}) copy-start(bf16[192,384]{1,0:T(8,128)(2,1)} %in_w.1) | copy-start | bytes 442372
  4.9 0.9 %copy-start.2 = (bf16[384,192]{0,1:T(8,128)(2,1)S(1)}, bf16[384,192]{0,1:T(8,128)(2,1)}, u32[]{:S(2)}) copy-start(bf16[384,192]{0,1:T(8,128)(2,1)} %param.10) | copy-start | bytes 442372
  12.8 1.1 %copy-start.13 = (pred[260,20]{0,1:T(8,128)(4,1)}, pred[260,20]{0,1:T(8,128)(4,1)S(1)}, u32[]{:S(2)}) copy-start(pred[260,20]{0,1:T(8,128)(4,1)S(1)} %concatenate.38) | copy-start | bytes 15604
  15.4 0.7 copy-start.5
  17.0 4.7 %collective-permute-start = (bf16[128,384]{1,0:T(8,128)(2,1)S(1)}, bf16[128,384]{1,0:T(8,128)(2,1)S(1)}, u32[]{:S(2)}, u32[]{:S(2)}) collective-permute-start(bf16[128,384]{1,0:T(8,128)(2,1)S(1)} %fusion.49), channel_id=1, source_target_pairs={{0,1},{1,0},{2,3},{3,2},{4,5},{5,4},{6,7},{7,6},{8,9},{9,8},{10,11... | collective-permute-start | bytes 294920 | tf_op jit(solution)/shard_map/ppermute | solution.py:17
  22.5 1.6 %copy-start.11 = (f32[256,384]{1,0:T(8,128)}, f32[256,384]{1,0:T(8,128)S(1)}, u32[]{:S(2)}) copy-start(f32[256,384]{1,0:T(8,128)S(1)} %fusion.81) | copy-start | bytes 1179652
  22.9 13.6 %collective-permute-start.1 = (bf16[128,384]{1,0:T(8,128)(2,1)S(1)}, bf16[128,384]{1,0:T(8,128)(2,1)}, u32[]{:S(2)}, u32[]{:S(2)}) collective-permute-start(bf16[128,384]{1,0:T(8,128)(2,1)S(1)} %slice.247), channel_id=1, source_target_pairs={{0,1},{1,0},{2,3},{3,2},{4,5},{5,4},{6,7},{7,6},{8,9},{9,8},{10,11... | collective-permute-start | bytes 294920 | tf_op jit(solution)/shard_map/ppermute | solution.py:17
  24.4 4.7 %collective-permute-start.2 = (bf16[128,384]{1,0:T(8,128)(2,1)S(1)}, bf16[128,384]{1,0:T(8,128)(2,1)S(1)}, u32[]{:S(2)}, u32[]{:S(2)}) collective-permute-start(bf16[128,384]{1,0:T(8,128)(2,1)S(1)} %slice.246), channel_id=1, source_target_pairs={{0,1},{1,0},{2,3},{3,2},{4,5},{5,4},{6,7},{7,6},{8,9},{9,8},{10,11... | collective-permute-start | bytes 294920 | tf_op jit(solution)/shard_map/ppermute | solution.py:17
  25.7 4.0 %copy-start.4 = (bf16[1,256,384]{2,1,0:T(8,128)(2,1)S(1)}, bf16[1,256,384]{2,1,0:T(8,128)(2,1)}, u32[]{:S(2)}) copy-start(bf16[1,256,384]{2,1,0:T(8,128)(2,1)} %param.11) | copy-start | bytes 589828
  33.4 3.1 %copy-start.12 = (f32[256,384]{1,0:T(8,128)S(1)}, f32[256,384]{1,0:T(8,128)}, u32[]{:S(2)}) copy-start(f32[256,384]{1,0:T(8,128)} %copy-done.11) | copy-start | bytes 1179652
  36.4 3.9 %copy-start.6 = (bf16[256,384]{1,0:T(8,128)(2,1)S(1)}, bf16[256,384]{1,0:T(8,128)(2,1)}, u32[]{:S(2)}) copy-start(bf16[256,384]{1,0:T(8,128)(2,1)} %copy-done.5) | copy-start | bytes 589828
  40.3 5.4 %copy-start.10 = (bf16[384,384]{1,0:T(8,128)(2,1)S(1)}, bf16[384,384]{1,0:T(8,128)(2,1)}, u32[]{:S(2)}) copy-start(bf16[384,384]{1,0:T(8,128)(2,1)} %convolution_convert_fusion.5) | copy-start | bytes 884740
  40.3 5.5 %copy-start.9 = (bf16[384,384]{1,0:T(8,128)(2,1)S(1)}, bf16[384,384]{1,0:T(8,128)(2,1)}, u32[]{:S(2)}) copy-start(bf16[384,384]{1,0:T(8,128)(2,1)} %convolution_convert_fusion.4) | copy-start | bytes 884740
  40.3 5.5 %copy-start.8 = (bf16[384,384]{1,0:T(8,128)(2,1)S(1)}, bf16[384,384]{1,0:T(8,128)(2,1)}, u32[]{:S(2)}) copy-start(bf16[384,384]{1,0:T(8,128)(2,1)} %convolution_convert_fusion.3) | copy-start | bytes 884740
  40.3 5.6 %copy-start.7 = (bf16[384,384]{1,0:T(8,128)(2,1)S(1)}, bf16[384,384]{1,0:T(8,128)(2,1)}, u32[]{:S(2)}) copy-start(bf16[384,384]{1,0:T(8,128)(2,1)} %convolution_convert_fusion.2) | copy-start | bytes 884740
  42.1 3.9 %collective-permute-start.4 = (bf16[2,384]{1,0:T(2,128)(2,1)S(1)}, bf16[2,384]{1,0:T(2,128)(2,1)S(1)}, u32[]{:S(2)}, u32[]{:S(2)}) collective-permute-start(bf16[2,384]{1,0:T(2,128)(2,1)S(1)} %get-tuple-element.22), channel_id=1, source_target_pairs={{0,2},{1,3},{4,6},{5,7},{8,10},{9,11},{12,14},{13,15},{16,18},{17,... | collective-permute-start | bytes 4616 | tf_op jit(solution)/shard_map/ppermute | solution.py:28
  43.4 3.0 %collective-permute-start.3 = (bf16[2,384]{1,0:T(2,128)(2,1)S(1)}, bf16[2,384]{1,0:T(2,128)(2,1)S(1)}, u32[]{:S(2)}, u32[]{:S(2)}) collective-permute-start(bf16[2,384]{1,0:T(2,128)(2,1)S(1)} %get-tuple-element.21), channel_id=1, source_target_pairs={{2,0},{3,1},{6,4},{7,5},{10,8},{11,9},{14,12},{15,13},{18,16},{19,... | collective-permute-start | bytes 4616 | tf_op jit(solution)/shard_map/ppermute | solution.py:30
  46.0 1.1 %copy-start.3 = (bf16[5,2,192,384]{3,2,0,1:T(8,128)(2,1)}, bf16[5,2,192,384]{3,2,0,1:T(8,128)(2,1)S(1)}, u32[]{:S(2)}) copy-start(bf16[5,2,192,384]{3,2,0,1:T(8,128)(2,1)S(1)} %constant_dynamic-update-slice_fusion) | copy-start | bytes 4423684
  46.8 0.7 copy-start.14
